TPU v7x, 32 devices: a whole 2x2x4 slice. The times are simulated.
32 devices in a mesh: rep: 2 (over x), node: 4 (over y, core), local: 4 (over z).
Axes of the slice: x: 2, y: 2, z: 4, core: 2. Of those that a mesh axis runs over, the one named last changes fastest.
Arguments:
- tokens: bfloat16 [512, 4096], P(('rep', 'node', 'local')), may hold values from -6 to 6
- expert_ids: int32 [512, 8], P(('rep', 'node', 'local')), may hold values from 0 to 15, all different within a row; in each aligned block of 16 rows (0 to 15, 16 to 31, ...) at most 16 rows name the same one
- route_weights: float32 [512, 8], P(('rep', 'node', 'local')), may hold values from 0.1 to 1
- gate_weight: bfloat16 [16, 768, 4096], P(('node', 'local'), 'rep'), may hold values from -0.09375 to 0.09375
- up_weight: bfloat16 [16, 768, 4096], P(('node', 'local'), 'rep'), may hold values from -0.09375 to 0.09375
- down_weight: bfloat16 [16, 768, 4096], P(('node', 'local'), None, 'rep'), may hold values from -0.21875 to 0.21875
Outputs:
- mixed_rows: bfloat16 [512, 4096], P(('rep', 'node', 'local'))
Inputs may be any that keep to these rules, and one draw needn't show every extreme that they name: `expert_ids`: each row names 8 different experts. Among the rows of one device (aligned blocks of 16 rows) no expert is named by more than 16 rows, and in some blocks some expert is named by exactly 16 rows.
All inputs are finite; a program needn't handle non-finite values.
Results may differ from a plain program's by a relative error of at most 0.0057.
Values may be sent and summed in bfloat16 or wider, within the bound.
No kernel may reach another device: no remote copies, remote signals or barrier semaphores. Data moves between devices by JAX's collectives and lax.ppermute only.
A program may use at most 64 MiB of HBM per device.

v0:
```python
import functools
import math

import jax
import jax.numpy as jnp
from jax import lax
from jax.experimental import pallas as pl
from jax.experimental.pallas import tpu as pltpu
from jax.sharding import PartitionSpec as P

PLANE = ("node", "local")
EVERY = ("rep", "node", "local")


def slot_table(expert_ids, expert_count, slot_cap):
    row_count, top_count = expert_ids.shape
    flat_ids = expert_ids.reshape(-1)
    hits = (flat_ids[:, None] == jnp.arange(expert_count, dtype=jnp.int32)[None, :]).astype(
        jnp.int32
    )
    before = jnp.cumsum(hits, axis=0) - hits
    rank_of = jnp.sum(before * hits, axis=1)
    return (flat_ids * slot_cap + rank_of).reshape(row_count, top_count)


def route_slots(blocks):
    return lax.all_to_all(blocks, PLANE, split_axis=1, concat_axis=1, tiled=True)


def by_slots(tokens, expert_ids, route_weights, gate_local, up_local, down_local, slot_cap):
    model_width = tokens.shape[1]
    plane_count = lax.axis_size("rep")
    expert_count = lax.axis_size("node") * lax.axis_size("local")
    slot_total = expert_count * slot_cap
    slot_of = slot_table(expert_ids, expert_count, slot_cap)
    slot_iota = jnp.arange(slot_total, dtype=jnp.int32)
    placed = jnp.any(slot_of[None, :, :] == slot_iota[:, None, None], axis=2).astype(jnp.bfloat16)
    outgoing = jnp.dot(placed, tokens, preferred_element_type=jnp.float32).astype(jnp.bfloat16)
    mixing = jnp.sum(
        jnp.where(slot_of[:, :, None] == slot_iota[None, None, :], route_weights[:, :, None], 0.0),
        axis=1,
    )
    arrived = route_slots(outgoing.reshape(1, expert_count, slot_cap, model_width))
    arrived = arrived.reshape(slot_total, model_width)
    shard_piece = lax.all_gather(arrived, "rep", axis=0, tiled=True)
    hidden_part = hidden_units(shard_piece, gate_local, up_local)
    expert_out = jnp.dot(
        lax.all_gather(hidden_part, "rep", axis=1, tiled=True),
        down_local,
        preferred_element_type=jnp.float32,
    ).astype(jnp.bfloat16)
    own_slots = lax.all_to_all(
        expert_out.reshape(plane_count, slot_total, down_local.shape[1]),
        "rep",
        split_axis=0,
        concat_axis=2,
        tiled=True,
    )
    returned = route_slots(own_slots.reshape(1, expert_count, slot_cap, model_width))
    back_rows = returned.reshape(slot_total, model_width).astype(jnp.float32)
    mixed_rows = jnp.dot(mixing, back_rows, precision=lax.Precision.HIGHEST)
    return mixed_rows.astype(jnp.bfloat16)


def hidden_units(rows, gate_local, up_local):
    feature_dims = (((1,), (1,)), ((), ()))
    gate = lax.dot_general(rows, gate_local, feature_dims, preferred_element_type=jnp.float32)
    up = lax.dot_general(rows, up_local, feature_dims, preferred_element_type=jnp.float32)
    return (jax.nn.silu(gate) * up).astype(jnp.bfloat16)


def swap(block, axes, mask):
    size = lax.axis_size(axes)
    return lax.ppermute(block, axes, [(place, place ^ mask) for place in range(size)])


def turn(block, first):
    nodes, size = lax.axis_size("node"), lax.axis_size(("rep", "node"))
    mask_of = [2 if (place % 2 == 0) == first else nodes for place in range(size)]
    pairs = [(place, place ^ mask) for place, mask in enumerate(mask_of)]
    return lax.ppermute(block, ("rep", "node"), pairs)


def square(block):
    side = turn(block, True)
    other_side = turn(block, False)
    return [side, turn(side, False), other_side, block]


def wide(block):
    return block.astype(jnp.float32)


def narrow(block):
    return block.astype(jnp.bfloat16)


def pack_kernel(tokens_in, ids_in, weights_in, out_ref, ids_ref, weights_ref, sems, *, experts):
    row_count, width = tokens_in.shape
    tokens_copy = pltpu.make_async_copy(tokens_in, out_ref.at[:, pl.ds(0, width)], sems.at[0])
    ids_copy = pltpu.make_async_copy(ids_in, ids_ref, sems.at[1])
    weights_copy = pltpu.make_async_copy(weights_in, weights_ref, sems.at[2])
    tokens_copy.start()
    ids_copy.start()
    weights_copy.start()
    extra = out_ref.shape[1] - width
    expert = lax.broadcasted_iota(jnp.int32, (extra, row_count), 0) % experts
    share = jnp.zeros(expert.shape, jnp.float32)
    ids_copy.wait()
    weights_copy.wait()
    for k in range(ids_ref.shape[0]):
        share += jnp.where(ids_ref[k : k + 1, :] == expert, weights_ref[k : k + 1, :], 0.0)
    share = jnp.concatenate([share, jnp.zeros((extra, extra - row_count), jnp.float32)], axis=1)
    share = share.T[:row_count]
    piece = lax.broadcasted_iota(jnp.int32, share.shape, 1) // experts
    high = wide(narrow(share))
    middle = wide(narrow(share - high))
    low = share - high - middle
    coded = jnp.where(piece == 0, high, jnp.where(piece == 1, middle, low))
    out_ref[:, width:] = narrow(jnp.where(piece < 3, coded, 0.0))
    tokens_copy.wait()


def fetch_kernel(*refs):
    *parts, out_ref, sems = refs
    row, copies = 0, []
    for place, part in enumerate(parts):
        rows = part.shape[0]
        there = out_ref.at[pl.ds(row, rows), :]
        copies.append(pltpu.make_async_copy(part, there, sems.at[place]))
        copies[-1].start()
        row += rows
    for copy in copies:
        copy.wait()


def gate_up_kernel(*refs, experts, starts, row_count, chunks):
    rows, out_refs = refs[-1], refs[-1 - 2 * chunks : -1]
    block_refs, weight_refs = refs[: len(starts)], refs[len(starts) : len(starts) + 2]
    part_width, width = weight_refs[0].shape[0] // 2, weight_refs[0].shape[1]
    own = lax.axis_index("node") * lax.axis_size("local") + lax.axis_index("local")
    other = own + lax.axis_size("local") * (1 - 2 * (lax.axis_index("node") % 2))
    lanes = lax.broadcasted_iota(jnp.int32, (row_count, block_refs[0].shape[1] - width), 1)
    coded = [
        (lanes % experts == expert) & (lanes < 3 * experts) for expert in (own, other)
    ]
    each = len(starts) // chunks
    core = lax.axis_index("node") % 2
    for place, (block, start) in enumerate(zip(block_refs, starts)):
        there = slice(start, start + row_count)
        chunk, (side, inner) = place // each, divmod(place % each, each // 4)
        if side in (1, 2):
            side = jnp.where(core == 0, side, 3 - side)
        first = pl.multiple_of((side * (each // 4) + inner) * row_count, row_count)
        rows[pl.ds(first + chunk * each * row_count, row_count), :] = block[there, :width]
        pieces = wide(block[there, width:])
        share_ref = out_refs[chunks + chunk]
        for expert in range(2):
            share = jnp.sum(jnp.where(coded[expert], pieces, 0.0), axis=1, keepdims=True)
            share = jnp.broadcast_to(share, (row_count, share_ref.shape[2]))
            share_ref[expert, pl.ds(first, row_count), :] = share
    feature_dims = (((1,), (1,)), ((), ()))
    for side, weights in enumerate(weight_refs):
        both = lax.dot_general(
            weights[...], rows[...], feature_dims, preferred_element_type=jnp.float32
        )
        gate, up = both[:part_width], both[part_width:]
        hidden = narrow((gate * up / (1.0 + jnp.exp(-gate))).T)
        for chunk, hidden_ref in enumerate(out_refs[:chunks]):
            total = hidden_ref.shape[1]
            hidden_ref[side] = hidden[chunk * total : (chunk + 1) * total]


def down_kernel(own_ref, other_ref, share_ref, down_own, down_other, *out_refs, quarters):
    plane = lax.axis_index("rep")
    width = down_own.shape[1]
    tile = math.gcd(width, 512)
    total = own_ref.shape[1]
    half, quarter = total // 2, total // 4
    hidden = []
    for side in range(2):
        own = own_ref[side]
        other = jnp.concatenate([other_ref[side, half:], other_ref[side, :half]], axis=0)
        first = jnp.where(plane == 0, own, other)
        second = jnp.where(plane == 0, other, own)
        hidden.append(jnp.concatenate([first, second], axis=1))
    for start in range(0, width, tile):
        here = slice(start, start + tile)
        term = 0.0
        for side, part in enumerate((down_own, down_other)):
            out = jnp.dot(hidden[side], part[:, here], preferred_element_type=jnp.float32)
            term += share_ref[side, :, :1] * wide(narrow(out))
        for out_ref, places in zip(out_refs, quarters):
            rows = [term[place * quarter : (place + 1) * quarter] for place in places]
            out_ref[:, here] = jnp.concatenate(rows, axis=0).astype(out_ref.dtype)


def run(kernel, operands, in_hbm, out_shape, scratch_shapes, flops, room=24, **sizes):
    held, fetched = pl.BlockSpec(memory_space=pltpu.VMEM), pl.BlockSpec(memory_space=pltpu.HBM)
    moved = sum(operand.size * operand.dtype.itemsize for operand in operands)
    return pl.pallas_call(
        functools.partial(kernel, **sizes),
        out_shape=out_shape,
        in_specs=[fetched if place in in_hbm else held for place in range(len(operands))],
        out_specs=jax.tree.map(lambda _: held, out_shape),
        scratch_shapes=scratch_shapes,
        compiler_params=pltpu.CompilerParams(vmem_limit_bytes=room * 1024 * 1024),
        cost_estimate=pl.CostEstimate(flops=flops, bytes_accessed=moved, transcendentals=0),
    )(*operands)


def pack(tokens, expert_ids, route_weights, experts):
    row_count, width = tokens.shape
    extra = -(-3 * experts // 128) * 128
    return run(
        pack_kernel,
        (tokens, expert_ids.T, route_weights.T),
        (0, 1, 2),
        jax.ShapeDtypeStruct((row_count, width + extra), jnp.bfloat16),
        [
            pltpu.VMEM(expert_ids.shape[::-1], jnp.int32),
            pltpu.VMEM(route_weights.shape[::-1], jnp.float32),
            pltpu.SemaphoreType.DMA((3,)),
        ],
        0,
        room=60,
        experts=experts,
    )


def fetch(arrays):
    rows = sum(array.shape[0] for array in arrays)
    return run(
        fetch_kernel,
        arrays,
        range(len(arrays)),
        jax.ShapeDtypeStruct((rows, arrays[0].shape[1]), arrays[0].dtype),
        [pltpu.SemaphoreType.DMA((len(arrays),))],
        0,
    )


def gate_up(parts, row_count, weights, experts):
    part_width, width = weights[0].shape[0] // 2, weights[0].shape[1]
    blocks, starts = zip(*(block for part in parts for block in part))
    total, chunks = len(blocks) * row_count, len(parts)
    outs = run(
        gate_up_kernel,
        (*blocks, *weights),
        (),
        [jax.ShapeDtypeStruct((2, total // chunks, part_width), jnp.bfloat16)] * chunks
        + [jax.ShapeDtypeStruct((2, total // chunks, 128), jnp.float32)] * chunks,
        [pltpu.VMEM((total, width), jnp.bfloat16)],
        8 * total * width * part_width,
        experts=experts,
        starts=starts,
        row_count=row_count,
        chunks=chunks,
    )
    return list(zip(outs[:chunks], outs[chunks:]))


def down(own, other, share, weights, quarters):
    total = own.shape[1]
    depth, width = weights[0].shape
    sizes = [(len(places) * total // 4, width) for places in quarters]
    return run(
        down_kernel,
        (own, other, share, *weights),
        (),
        [jax.ShapeDtypeStruct(sizes[0], jnp.float32)]
        + [jax.ShapeDtypeStruct(size, jnp.bfloat16) for size in sizes[1:]],
        [],
        4 * total * depth * width,
        quarters=quarters,
    )


def by_rows(tokens, expert_ids, route_weights, gate_local, up_local, down_local):
    row_count = tokens.shape[0]
    experts = lax.axis_size("node") * lax.axis_size("local")
    places = lax.axis_size("local")
    plane = lax.axis_index("rep")
    together = lax.optimization_barrier

    packed = pack(tokens, expert_ids, route_weights, experts)
    line_3, line_1, square_0, gates = together(
        (
            swap(packed, "local", 3),
            swap(packed, "local", 1),
            square(packed),
            fetch((gate_local, up_local)),
        )
    )
    other_gates = swap(gates, "node", 1)
    block_13 = jnp.concatenate([line_1, line_3], axis=0)
    side_13, other_13, line_2 = turn(block_13, True), turn(block_13, False), swap(line_3, "local", 1)
    line_2, side_13, other_13, downs = together((line_2, side_13, other_13, fetch((down_local,))))
    square_13 = [side_13, turn(side_13, False), other_13, block_13]

    def hidden_of(*parts):
        order = (3, 0, 2, 1)
        blocks = [(square[side], row) for side in order for square, row in parts]
        return gate_up((blocks,), row_count, (gates, other_gates), experts)[0]

    def exchanged(hidden, share):
        return hidden, swap(hidden, "rep", 1), share

    hidden_b = hidden_of((square_13, 0), (square_13, row_count))
    hidden_b, square_2, other_downs = together(
        (hidden_b, square(line_2), swap(downs, "node", 1))
    )
    weights = (downs, other_downs)
    hidden_a = hidden_of((square_0, 0), (square_2, 0))
    hidden_b, hidden_a = exchanged(*hidden_b), exchanged(*hidden_a)
    keep, send_y = down(*hidden_b, weights, ((0, 2), (1, 3)))
    back_y = swap(send_y, "node", 2)
    keep_a, send_y, send_x, send_across = down(*hidden_a, weights, ((0,), (1,), (2,), (3,)))
    across = swap(send_across, ("rep", "node"), lax.axis_size("node") | 2)
    along_x, along_y = swap(send_x, "rep", 1), swap(send_y, "node", 2)
    here, there = narrow(keep + wide(back_y)).reshape(2, 2 * row_count, -1)
    there = swap(there, ("rep", "local"), places | 1)
    here = swap(here, "local", 1)
    own = keep_a + wide(along_y) + wide(here)
    other = wide(along_x) + wide(across) + wide(there)
    total = jnp.stack([own, other]).reshape(2, 2, row_count, -1)
    own, other = narrow(total[:, 0] + wide(swap(narrow(total[:, 1]), "local", 2)))
    return jnp.where(
        plane == 0,
        jnp.concatenate([own, other], axis=1),
        jnp.concatenate([other, own], axis=1),
    )


def on_device(tokens, expert_ids, route_weights, gate_weight, up_weight, down_weight):
    row_count, top_count = expert_ids.shape
    expert_count = lax.axis_size("node") * lax.axis_size("local")
    slot_cap = min(row_count, max(2, 2 * row_count * top_count // expert_count))
    weights = (gate_weight[0], up_weight[0], down_weight[0])
    if slot_cap == row_count:
        return by_rows(tokens, expert_ids, route_weights, *weights)
    return by_slots(tokens, expert_ids, route_weights, *weights, slot_cap)


def solution(mesh):
    placed = (
        P(EVERY, None),
        P(EVERY, None),
        P(EVERY, None),
        P(PLANE, "rep", None),
        P(PLANE, "rep", None),
        P(PLANE, None, "rep"),
    )
    return jax.shard_map(
        on_device,
        mesh=mesh,
        in_specs=placed,
        out_specs=P(EVERY, None),
        check_vma=False,
    )
```

profile of v0, /device:TPU:0, one launch (start us, length us, event | category | flops | bytes accessed | tf_op | source)
XLA Modules:
  0.0 67.4 jit_solution(1092098500087412529)
XLA Ops:
  0.0 1.6 %shard_map.64.refs_0_ = bf16[16,4224]{1,0:T(8,128)(2,1)} custom-call(bf16[16,4096]{1,0:T(8,128)(2,1)} %tokens_in.1, s32[8,16]{1,0:T(8,128)} %bitcast.30, f32[8,16]{1,0:T(8,128)} %bitcast.31), custom_call_target="tpu_custom_call" | custom-call | bytes 132096 | tf_op jit(solution)/shard_map/pallas_call | solution.py:201
  1.6 3.0 %collective-permute-start.2 = (bf16[16,4224]{1,0:T(8,128)(2,1)}, bf16[16,4224]{1,0:T(8,128)(2,1)S(1)}, u32[]{:S(2)}, u32[]{:S(2)}) collective-permute-start(bf16[16,4224]{1,0:T(8,128)(2,1)} %shard_map.64.refs_0_), channel_id=1, source_target_pairs={{0,8},{4,20},{8,0},{12,28},{16,24},{20,4},{24,16},{28,12},{1,9},{5... | collective-permute-start | bytes 405512 | tf_op jit(solution)/shard_map/ppermute | solution.py:81
  4.6 3.6 %collective-permute-start = (bf16[16,4224]{1,0:T(8,128)(2,1)}, bf16[16,4224]{1,0:T(8,128)(2,1)S(1)}, u32[]{:S(2)}, u32[]{:S(2)}) collective-permute-start(bf16[16,4224]{1,0:T(8,128)(2,1)} %shard_map.64.refs_0_), channel_id=1, source_target_pairs={{0,3},{1,2},{2,1},{3,0},{4,7},{5,6},{6,5},{7,4},{8,11},{9,10},{10,... | collective-permute-start | bytes 405512 | tf_op jit(solution)/shard_map/ppermute | solution.py:74
  8.2 0.0 collective-permute-start.1
  8.2 1.5 %collective-permute-start.4 = (bf16[16,4224]{1,0:T(8,128)(2,1)}, bf16[16,4224]{1,0:T(8,128)(2,1)S(1)}, u32[]{:S(2)}, u32[]{:S(2)}) collective-permute-start(bf16[16,4224]{1,0:T(8,128)(2,1)} %shard_map.64.refs_0_), channel_id=1, source_target_pairs={{0,16},{4,12},{8,24},{12,4},{16,0},{20,28},{24,8},{28,20},{1,17},{... | collective-permute-start | bytes 405512 | tf_op jit(solution)/shard_map/ppermute | solution.py:81
  9.7 0.0 collective-permute-done.2.refs_2_
  9.7 0.5 collective-permute-start.3
  10.3 1.9 %copy-done.1 = bf16[1,384,4096]{2,1,0:T(8,128)(2,1)S(1)} copy-done((bf16[1,384,4096]{2,1,0:T(8,128)(2,1)S(1)}, bf16[1,384,4096]{2,1,0:T(8,128)(2,1)}, u32[]{:S(2)}) %copy-start.1) | copy-done | bytes 3145752
  12.2 1.9 %copy-done.2 = bf16[1,384,4096]{2,1,0:T(8,128)(2,1)S(1)} copy-done((bf16[1,384,4096]{2,1,0:T(8,128)(2,1)S(1)}, bf16[1,384,4096]{2,1,0:T(8,128)(2,1)}, u32[]{:S(2)}) %copy-start.2) | copy-done | bytes 3145752
  14.0 0.4 shard_map.65.refs_8_
  14.5 0.0 collective-permute-done
  14.5 0.2 collective-permute-done.1
  14.7 0.2 collective-permute-done.3.refs_6_
  14.9 1.5 %collective-permute-start.6 = (bf16[32,4224]{1,0:T(8,128)(2,1)S(1)}, bf16[32,4224]{1,0:T(8,128)(2,1)S(1)}, u32[]{:S(2)}, u32[]{:S(2)}) collective-permute-start(bf16[32,4224]{1,0:T(8,128)(2,1)S(1)} %constant_dynamic-update-slice_fusion.refs_0_.refs_1_), channel_id=1, source_target_pairs={{0,8},{4,20},{8,0},{12,28},{16,24},{20,4},{24,16},{28,12},{1,9},{5... | collective-permute-start | bytes 811016 | tf_op jit(solution)/shard_map/ppermute | solution.py:81
  16.4 0.6 collective-permute-start.7
  17.0 2.0 %collective-permute-start.5 = (bf16[16,4224]{1,0:T(8,128)(2,1)S(1)}, bf16[16,4224]{1,0:T(8,128)(2,1)S(1)}, u32[]{:S(2)}, u32[]{:S(2)}) collective-permute-start(bf16[16,4224]{1,0:T(8,128)(2,1)S(1)} %collective-permute-done), channel_id=1, source_target_pairs={{0,1},{1,0},{2,3},{3,2},{4,5},{5,4},{6,7},{7,6},{8,9},{9,8},{10,11... | collective-permute-start | bytes 405512 | tf_op jit(solution)/shard_map/ppermute | solution.py:74
  19.0 0.2 shard_map.66.down_own
  19.3 3.5 %collective-permute-done.5.refs_1_ = bf16[16,4224]{1,0:T(8,128)(2,1)S(1)} collective-permute-done((bf16[16,4224]{1,0:T(8,128)(2,1)S(1)}, bf16[16,4224]{1,0:T(8,128)(2,1)S(1)}, u32[]{:S(2)}, u32[]{:S(2)}) %collective-permute-start.5) | collective-permute-done | bytes 135200 | tf_op jit(solution)/shard_map/ppermute | solution.py:74
  22.7 0.9 %collective-permute-done.6.refs_2_.refs_3_ = bf16[32,4224]{1,0:T(8,128)(2,1)S(1)} collective-permute-done((bf16[32,4224]{1,0:T(8,128)(2,1)S(1)}, bf16[32,4224]{1,0:T(8,128)(2,1)S(1)}, u32[]{:S(2)}, u32[]{:S(2)}) %collective-permute-start.6) | collective-permute-done | bytes 270368 | tf_op jit(solution)/shard_map/ppermute | solution.py:81
  23.6 0.2 collective-permute-done.7.refs_4_.refs_5_
  23.9 0.3 collective-permute-start.13
  24.2 1.5 %collective-permute-start.8 = (bf16[32,4224]{1,0:T(8,128)(2,1)S(1)}, bf16[32,4224]{1,0:T(8,128)(2,1)S(1)}, u32[]{:S(2)}, u32[]{:S(2)}) collective-permute-start(bf16[32,4224]{1,0:T(8,128)(2,1)S(1)} %collective-permute-done.6.refs_2_.refs_3_), channel_id=1, source_target_pairs={{0,16},{4,12},{8,24},{12,4},{16,0},{20,28},{24,8},{28,20},{1,17},{... | collective-permute-start | bytes 811016 | tf_op jit(solution)/shard_map/ppermute | solution.py:81
  25.7 0.5 collective-permute-start.10
  26.2 1.5 %collective-permute-start.12 = (bf16[16,4224]{1,0:T(8,128)(2,1)S(1)}, bf16[16,4224]{1,0:T(8,128)(2,1)S(1)}, u32[]{:S(2)}, u32[]{:S(2)}) collective-permute-start(bf16[16,4224]{1,0:T(8,128)(2,1)S(1)} %collective-permute-done.5.refs_1_), channel_id=1, source_target_pairs={{0,16},{4,12},{8,24},{12,4},{16,0},{20,28},{24,8},{28,20},{1,17},{... | collective-permute-start | bytes 405512 | tf_op jit(solution)/shard_map/ppermute | solution.py:81
  27.6 4.5 %collective-permute-done.10.refs_3_ = bf16[16,4224]{1,0:T(8,128)(2,1)S(1)} collective-permute-done((bf16[16,4224]{1,0:T(8,128)(2,1)S(1)}, bf16[16,4224]{1,0:T(8,128)(2,1)S(1)}, u32[]{:S(2)}, u32[]{:S(2)}) %collective-permute-start.10) | collective-permute-done | bytes 135200 | tf_op jit(solution)/shard_map/ppermute | solution.py:81
  32.2 0.5 collective-permute-start.11
  32.7 3.5 %shard_map.67 = (bf16[2,128,384]{2,1,0:T(8,128)(2,1)S(1)}, f32[2,128,128]{2,1,0:T(8,128)S(1)}) custom-call(bf16[32,4224]{1,0:T(8,128)(2,1)S(1)} %constant_dynamic-update-slice_fusion.refs_0_.refs_1_, bf16[32,4224]{1,0:T(8,128)(2,1)S(1)} %constant_dynamic-update-slice_fusion.refs_0_.refs_1_, bf16[32,4224]{1,0:T(8,128)(2,1)S(1)} %collective-permute-done.6.refs_2_.refs_3_, ...), custom_call_target="tpu_custom_call" | custom-call | flops 1610612736 | bytes 14745600 | tf_op jit(solution)/shard_map/pallas_call | solution.py:201
  36.2 1.0 %collective-permute-done.11.refs_7_ = bf16[16,4224]{1,0:T(8,128)(2,1)S(1)} collective-permute-done((bf16[16,4224]{1,0:T(8,128)(2,1)S(1)}, bf16[16,4224]{1,0:T(8,128)(2,1)S(1)}, u32[]{:S(2)}, u32[]{:S(2)}) %collective-permute-start.11) | collective-permute-done | bytes 135200 | tf_op jit(solution)/shard_map/ppermute | solution.py:81
  37.2 0.6 collective-permute-start.16
  37.8 3.5 %shard_map.68 = (bf16[2,128,384]{2,1,0:T(8,128)(2,1)S(1)}, f32[2,128,128]{2,1,0:T(8,128)S(1)}) custom-call(bf16[16,4224]{1,0:T(8,128)(2,1)S(1)} %copy-done.3, bf16[16,4224]{1,0:T(8,128)(2,1)S(1)} %collective-permute-done.5.refs_1_, bf16[16,4224]{1,0:T(8,128)(2,1)S(1)} %collective-permute-done.2.refs_2_, ...), custom_call_target="tpu_custom_call" | custom-call | flops 1610612736 | bytes 13664256 | tf_op jit(solution)/shard_map/pallas_call | solution.py:201
  41.3 1.5 %collective-permute-start.14 = (bf16[2,128,384]{2,1,0:T(8,128)(2,1)S(1)}, bf16[2,128,384]{2,1,0:T(8,128)(2,1)S(1)}, u32[]{:S(2)}, u32[]{:S(2)}) collective-permute-start(bf16[2,128,384]{2,1,0:T(8,128)(2,1)S(1)} %get-tuple-element.50.own_ref), channel_id=1, source_target_pairs={{0,16},{16,0},{1,17},{17,1},{2,18},{18,2},{3,19},{19,3},{4,20},{20... | collective-permute-start | bytes 589832 | tf_op jit(solution)/shard_map/ppermute | solution.py:74
  42.8 0.1 collective-permute-done.16.other_ref
  42.9 1.1 %shard_map.70 = (f32[64,2048]{1,0:T(8,128)S(1)}, bf16[64,2048]{1,0:T(8,128)(2,1)S(1)}) custom-call(bf16[2,128,384]{2,1,0:T(8,128)(2,1)S(1)} %get-tuple-element.55.own_ref, bf16[2,128,384]{2,1,0:T(8,128)(2,1)S(1)} %collective-permute-done.16.other_ref, f32[2,128,128]{2,1,0:T(8,128)S(1)} %get-tuple-element.56.share_ref, ...), custom_call_target="tpu_custom_call" | custom-call | flops 805306368 | bytes 6815744 | tf_op jit(solution)/shard_map/pallas_call | solution.py:201
  44.0 1.1 %collective-permute-start.17 = (bf16[64,2048]{1,0:T(8,128)(2,1)S(1)}, bf16[64,2048]{1,0:T(8,128)(2,1)S(1)}, u32[]{:S(2)}, u32[]{:S(2)}) collective-permute-start(bf16[64,2048]{1,0:T(8,128)(2,1)S(1)} %get-tuple-element.58), channel_id=1, source_target_pairs={{0,8},{4,12},{8,0},{12,4},{1,9},{5,13},{9,1},{13,5},{2,10},{6,14},... | collective-permute-start | bytes 786440 | tf_op jit(solution)/shard_map/ppermute | solution.py:74
  45.1 2.0 %collective-permute-done.14.other_ref = bf16[2,128,384]{2,1,0:T(8,128)(2,1)S(1)} collective-permute-done((bf16[2,128,384]{2,1,0:T(8,128)(2,1)S(1)}, bf16[2,128,384]{2,1,0:T(8,128)(2,1)S(1)}, u32[]{:S(2)}, u32[]{:S(2)}) %collective-permute-start.14) | collective-permute-done | bytes 196640 | tf_op jit(solution)/shard_map/ppermute | solution.py:74
  47.1 1.1 %shard_map.69 = (f32[32,2048]{1,0:T(8,128)S(1)}, bf16[32,2048]{1,0:T(8,128)(2,1)S(1)}, bf16[32,2048]{1,0:T(8,128)(2,1)S(1)}, bf16[32,2048]{1,0:T(8,128)(2,1)S(1)}) custom-call(bf16[2,128,384]{2,1,0:T(8,128)(2,1)S(1)} %get-tuple-element.50.own_ref, bf16[2,128,384]{2,1,0:T(8,128)(2,1)S(1)} %collective-permute-done.14.other_ref, ...), custom_call_target="tpu_custom_call" | custom-call | flops 805306368 | bytes 6815744 | tf_op jit(solution)/shard_map/pallas_call | solution.py:201
  48.1 1.5 %collective-permute-start.19 = (bf16[32,2048]{1,0:T(8,128)(2,1)S(1)}, bf16[32,2048]{1,0:T(8,128)(2,1)S(1)}, u32[]{:S(2)}, u32[]{:S(2)}) collective-permute-start(bf16[32,2048]{1,0:T(8,128)(2,1)S(1)} %get-tuple-element.59), channel_id=1, source_target_pairs={{0,16},{16,0},{1,17},{17,1},{2,18},{18,2},{3,19},{19,3},{4,20},{20... | collective-permute-start | bytes 393224 | tf_op jit(solution)/shard_map/ppermute | solution.py:74
  49.6 1.4 %collective-permute-start.20 = (bf16[32,2048]{1,0:T(8,128)(2,1)S(1)}, bf16[32,2048]{1,0:T(8,128)(2,1)S(1)}, u32[]{:S(2)}, u32[]{:S(2)}) collective-permute-start(bf16[32,2048]{1,0:T(8,128)(2,1)S(1)} %get-tuple-element.60), channel_id=1, source_target_pairs={{0,24},{4,28},{8,16},{12,20},{16,8},{20,12},{24,0},{28,4},{1,25},{... | collective-permute-start | bytes 393224 | tf_op jit(solution)/shard_map/ppermute | solution.py:74
  51.0 0.8 %collective-permute-done.17 = bf16[64,2048]{1,0:T(8,128)(2,1)S(1)} collective-permute-done((bf16[64,2048]{1,0:T(8,128)(2,1)S(1)}, bf16[64,2048]{1,0:T(8,128)(2,1)S(1)}, u32[]{:S(2)}, u32[]{:S(2)}) %collective-permute-start.17) | collective-permute-done | bytes 262176 | tf_op jit(solution)/shard_map/ppermute | solution.py:74
  51.9 3.1 %collective-permute-start.21 = (bf16[32,2048]{1,0:T(8,128)(2,1)S(1)}, bf16[32,2048]{1,0:T(8,128)(2,1)S(1)}, u32[]{:S(2)}, u32[]{:S(2)}) collective-permute-start(bf16[32,2048]{1,0:T(8,128)(2,1)S(1)} %get-tuple-element.61), channel_id=1, source_target_pairs={{0,17},{1,16},{2,19},{3,18},{16,1},{17,0},{18,3},{19,2},{4,21},{5,... | collective-permute-start | bytes 393224 | tf_op jit(solution)/shard_map/ppermute | solution.py:74
  55.1 0.4 collective-permute-start.18
  55.4 2.1 %collective-permute-done.20 = bf16[32,2048]{1,0:T(8,128)(2,1)S(1)} collective-permute-done((bf16[32,2048]{1,0:T(8,128)(2,1)S(1)}, bf16[32,2048]{1,0:T(8,128)(2,1)S(1)}, u32[]{:S(2)}, u32[]{:S(2)}) %collective-permute-start.20) | collective-permute-done | bytes 131104 | tf_op jit(solution)/shard_map/ppermute | solution.py:74
  57.5 0.5 collective-permute-done.21
  58.1 2.0 %collective-permute-done.15 = bf16[32,2048]{1,0:T(8,128)(2,1)S(1)} collective-permute-done((bf16[32,2048]{1,0:T(8,128)(2,1)S(1)}, bf16[32,2048]{1,0:T(8,128)(2,1)S(1)}, u32[]{:S(2)}, u32[]{:S(2)}) %collective-permute-start.15) | collective-permute-done | bytes 131104 | tf_op jit(solution)/shard_map/ppermute | solution.py:74
  60.0 0.6 collective-permute-done.18
  60.7 2.7 %collective-permute-start.22 = (bf16[2,16,2048]{2,1,0:T(8,128)(2,1)S(1)}, bf16[2,16,2048]{2,1,0:T(8,128)(2,1)S(1)}, u32[]{:S(2)}, u32[]{:S(2)}) collective-permute-start(bf16[2,16,2048]{2,1,0:T(8,128)(2,1)S(1)} %fusion.5), channel_id=1, source_target_pairs={{0,2},{1,3},{2,0},{3,1},{4,6},{5,7},{6,4},{7,5},{8,10},{9,11},{10,... | collective-permute-start | bytes 393224 | tf_op jit(solution)/shard_map/ppermute | solution.py:74
  63.4 3.2 %collective-permute-done.22 = bf16[2,16,2048]{2,1,0:T(8,128)(2,1)S(1)} collective-permute-done((bf16[2,16,2048]{2,1,0:T(8,128)(2,1)S(1)}, bf16[2,16,2048]{2,1,0:T(8,128)(2,1)S(1)}, u32[]{:S(2)}, u32[]{:S(2)}) %collective-permute-start.22) | collective-permute-done | bytes 131104 | tf_op jit(solution)/shard_map/ppermute | solution.py:74
  66.7 0.7 %maximum_select_fusion = bf16[16,4096]{1,0:T(8,128)(2,1)} fusion(bf16[16,2048]{1,0:T(8,128)(2,1)S(1)} %get-tuple-element.64, bf16[16,2048]{1,0:T(8,128)(2,1)S(1)} %get-tuple-element.63, pred[]{:T(512)S(6)} %eq.3), kind=kLoop, calls=%fused_computation.12 | loop fusion | flops 589824 | bytes 262145 | tf_op jit(solution)/shard_map/jit(_where)/select_n | solution.py:328
  (23 shorter events, 0.3 us)
Async XLA Ops:
  1.6 8.1 %collective-permute-start.2 = (bf16[16,4224]{1,0:T(8,128)(2,1)}, bf16[16,4224]{1,0:T(8,128)(2,1)S(1)}, u32[]{:S(2)}, u32[]{:S(2)}) collective-permute-start(bf16[16,4224]{1,0:T(8,128)(2,1)} %shard_map.64.refs_0_), channel_id=1, source_target_pairs={{0,8},{4,20},{8,0},{12,28},{16,24},{20,4},{24,16},{28,12},{1,9},{5... | collective-permute-start | bytes 405512 | tf_op jit(solution)/shard_map/ppermute | solution.py:81
  4.6 9.9 %collective-permute-start = (bf16[16,4224]{1,0:T(8,128)(2,1)}, bf16[16,4224]{1,0:T(8,128)(2,1)S(1)}, u32[]{:S(2)}, u32[]{:S(2)}) collective-permute-start(bf16[16,4224]{1,0:T(8,128)(2,1)} %shard_map.64.refs_0_), channel_id=1, source_target_pairs={{0,3},{1,2},{2,1},{3,0},{4,7},{5,6},{6,5},{7,4},{8,11},{9,10},{10,... | collective-permute-start | bytes 405512 | tf_op jit(solution)/shard_map/ppermute | solution.py:74
  8.2 6.5 %collective-permute-start.1 = (bf16[16,4224]{1,0:T(8,128)(2,1)}, bf16[16,4224]{1,0:T(8,128)(2,1)S(1)}, u32[]{:S(2)}, u32[]{:S(2)}) collective-permute-start(bf16[16,4224]{1,0:T(8,128)(2,1)} %shard_map.64.refs_0_), channel_id=1, source_target_pairs={{0,1},{1,0},{2,3},{3,2},{4,5},{5,4},{6,7},{7,6},{8,9},{9,8},{10,11... | collective-permute-start | bytes 405512 | tf_op jit(solution)/shard_map/ppermute | solution.py:74
  8.2 6.5 %collective-permute-start.4 = (bf16[16,4224]{1,0:T(8,128)(2,1)}, bf16[16,4224]{1,0:T(8,128)(2,1)S(1)}, u32[]{:S(2)}, u32[]{:S(2)}) collective-permute-start(bf16[16,4224]{1,0:T(8,128)(2,1)} %shard_map.64.refs_0_), channel_id=1, source_target_pairs={{0,16},{4,12},{8,24},{12,4},{16,0},{20,28},{24,8},{28,20},{1,17},{... | collective-permute-start | bytes 405512 | tf_op jit(solution)/shard_map/ppermute | solution.py:81
  9.7 5.2 %collective-permute-start.3 = (bf16[16,4224]{1,0:T(8,128)(2,1)S(1)}, bf16[16,4224]{1,0:T(8,128)(2,1)S(1)}, u32[]{:S(2)}, u32[]{:S(2)}) collective-permute-start(bf16[16,4224]{1,0:T(8,128)(2,1)S(1)} %collective-permute-done.2.refs_2_), channel_id=1, source_target_pairs={{0,16},{4,12},{8,24},{12,4},{16,0},{20,28},{24,8},{28,20},{1,17},{... | collective-permute-start | bytes 405512 | tf_op jit(solution)/shard_map/ppermute | solution.py:81
  10.3 1.9 %copy-start.1 = (bf16[1,384,4096]{2,1,0:T(8,128)(2,1)S(1)}, bf16[1,384,4096]{2,1,0:T(8,128)(2,1)}, u32[]{:S(2)}) copy-start(bf16[1,384,4096]{2,1,0:T(8,128)(2,1)} %param.9) | copy-start | bytes 9437188
  12.1 1.9 %copy-start.2 = (bf16[1,384,4096]{2,1,0:T(8,128)(2,1)S(1)}, bf16[1,384,4096]{2,1,0:T(8,128)(2,1)}, u32[]{:S(2)}) copy-start(bf16[1,384,4096]{2,1,0:T(8,128)(2,1)} %param.10) | copy-start | bytes 9437188
  14.0 5.0 %copy-start = (bf16[1,768,2048]{2,1,0:T(8,128)(2,1)S(1)}, bf16[1,768,2048]{2,1,0:T(8,128)(2,1)}, u32[]{:S(2)}) copy-start(bf16[1,768,2048]{2,1,0:T(8,128)(2,1)} %param.11) | copy-start | bytes 9437188
  14.9 17.8 %collective-permute-start.9 = (bf16[768,4096]{1,0:T(8,128)(2,1)S(1)}, bf16[768,4096]{1,0:T(8,128)(2,1)S(1)}, u32[]{:S(2)}, u32[]{:S(2)}) collective-permute-start(bf16[768,4096]{1,0:T(8,128)(2,1)S(1)} %shard_map.65.refs_8_), channel_id=1, source_target_pairs={{0,4},{4,0},{8,12},{12,8},{1,5},{5,1},{9,13},{13,9},{2,6},{6,2},{1... | collective-permute-start | bytes 18874376 | tf_op jit(solution)/shard_map/ppermute | solution.py:74
  14.9 8.7 %collective-permute-start.6 = (bf16[32,4224]{1,0:T(8,128)(2,1)S(1)}, bf16[32,4224]{1,0:T(8,128)(2,1)S(1)}, u32[]{:S(2)}, u32[]{:S(2)}) collective-permute-start(bf16[32,4224]{1,0:T(8,128)(2,1)S(1)} %constant_dynamic-update-slice_fusion.refs_0_.refs_1_), channel_id=1, source_target_pairs={{0,8},{4,20},{8,0},{12,28},{16,24},{20,4},{24,16},{28,12},{1,9},{5... | collective-permute-start | bytes 811016 | tf_op jit(solution)/shard_map/ppermute | solution.py:81
  16.4 7.5 %collective-permute-start.7 = (bf16[32,4224]{1,0:T(8,128)(2,1)S(1)}, bf16[32,4224]{1,0:T(8,128)(2,1)S(1)}, u32[]{:S(2)}, u32[]{:S(2)}) collective-permute-start(bf16[32,4224]{1,0:T(8,128)(2,1)S(1)} %constant_dynamic-update-slice_fusion.refs_0_.refs_1_), channel_id=1, source_target_pairs={{0,16},{4,12},{8,24},{12,4},{16,0},{20,28},{24,8},{28,20},{1,17},{... | collective-permute-start | bytes 811016 | tf_op jit(solution)/shard_map/ppermute | solution.py:81
  17.0 5.7 %collective-permute-start.5 = (bf16[16,4224]{1,0:T(8,128)(2,1)S(1)}, bf16[16,4224]{1,0:T(8,128)(2,1)S(1)}, u32[]{:S(2)}, u32[]{:S(2)}) collective-permute-start(bf16[16,4224]{1,0:T(8,128)(2,1)S(1)} %collective-permute-done), channel_id=1, source_target_pairs={{0,1},{1,0},{2,3},{3,2},{4,5},{5,4},{6,7},{7,6},{8,9},{9,8},{10,11... | collective-permute-start | bytes 405512 | tf_op jit(solution)/shard_map/ppermute | solution.py:74
  19.3 18.6 %copy-start.3 = (bf16[16,4224]{1,0:T(8,128)(2,1)S(1)}, bf16[16,4224]{1,0:T(8,128)(2,1)}, u32[]{:S(2)}) copy-start(bf16[16,4224]{1,0:T(8,128)(2,1)} %shard_map.64.refs_0_) | copy-start | bytes 405508
  23.9 13.3 %collective-permute-start.13 = (bf16[768,2048]{1,0:T(8,128)(2,1)S(1)}, bf16[768,2048]{1,0:T(8,128)(2,1)S(1)}, u32[]{:S(2)}, u32[]{:S(2)}) collective-permute-start(bf16[768,2048]{1,0:T(8,128)(2,1)S(1)} %shard_map.66.down_own), channel_id=1, source_target_pairs={{0,4},{4,0},{8,12},{12,8},{1,5},{5,1},{9,13},{13,9},{2,6},{6,2},{1... | collective-permute-start | bytes 9437192 | tf_op jit(solution)/shard_map/ppermute | solution.py:74
  24.2 8.5 %collective-permute-start.8 = (bf16[32,4224]{1,0:T(8,128)(2,1)S(1)}, bf16[32,4224]{1,0:T(8,128)(2,1)S(1)}, u32[]{:S(2)}, u32[]{:S(2)}) collective-permute-start(bf16[32,4224]{1,0:T(8,128)(2,1)S(1)} %collective-permute-done.6.refs_2_.refs_3_), channel_id=1, source_target_pairs={{0,16},{4,12},{8,24},{12,4},{16,0},{20,28},{24,8},{28,20},{1,17},{... | collective-permute-start | bytes 811016 | tf_op jit(solution)/shard_map/ppermute | solution.py:81
  25.7 6.5 %collective-permute-start.10 = (bf16[16,4224]{1,0:T(8,128)(2,1)S(1)}, bf16[16,4224]{1,0:T(8,128)(2,1)S(1)}, u32[]{:S(2)}, u32[]{:S(2)}) collective-permute-start(bf16[16,4224]{1,0:T(8,128)(2,1)S(1)} %collective-permute-done.5.refs_1_), channel_id=1, source_target_pairs={{0,8},{4,20},{8,0},{12,28},{16,24},{20,4},{24,16},{28,12},{1,9},{5... | collective-permute-start | bytes 405512 | tf_op jit(solution)/shard_map/ppermute | solution.py:81
  26.2 10.0 %collective-permute-start.12 = (bf16[16,4224]{1,0:T(8,128)(2,1)S(1)}, bf16[16,4224]{1,0:T(8,128)(2,1)S(1)}, u32[]{:S(2)}, u32[]{:S(2)}) collective-permute-start(bf16[16,4224]{1,0:T(8,128)(2,1)S(1)} %collective-permute-done.5.refs_1_), channel_id=1, source_target_pairs={{0,16},{4,12},{8,24},{12,4},{16,0},{20,28},{24,8},{28,20},{1,17},{... | collective-permute-start | bytes 405512 | tf_op jit(solution)/shard_map/ppermute | solution.py:81
  32.2 5.0 %collective-permute-start.11 = (bf16[16,4224]{1,0:T(8,128)(2,1)S(1)}, bf16[16,4224]{1,0:T(8,128)(2,1)S(1)}, u32[]{:S(2)}, u32[]{:S(2)}) collective-permute-start(bf16[16,4224]{1,0:T(8,128)(2,1)S(1)} %collective-permute-done.10.refs_3_), channel_id=1, source_target_pairs={{0,16},{4,12},{8,24},{12,4},{16,0},{20,28},{24,8},{28,20},{1,17},{... | collective-permute-start | bytes 405512 | tf_op jit(solution)/shard_map/ppermute | solution.py:81
  37.2 5.7 %collective-permute-start.16 = (bf16[2,128,384]{2,1,0:T(8,128)(2,1)S(1)}, bf16[2,128,384]{2,1,0:T(8,128)(2,1)S(1)}, u32[]{:S(2)}, u32[]{:S(2)}) collective-permute-start(bf16[2,128,384]{2,1,0:T(8,128)(2,1)S(1)} %get-tuple-element.55.own_ref), channel_id=1, source_target_pairs={{0,16},{16,0},{1,17},{17,1},{2,18},{18,2},{3,19},{19,3},{4,20},{20... | collective-permute-start | bytes 589832 | tf_op jit(solution)/shard_map/ppermute | solution.py:74
  41.3 5.7 %collective-permute-start.14 = (bf16[2,128,384]{2,1,0:T(8,128)(2,1)S(1)}, bf16[2,128,384]{2,1,0:T(8,128)(2,1)S(1)}, u32[]{:S(2)}, u32[]{:S(2)}) collective-permute-start(bf16[2,128,384]{2,1,0:T(8,128)(2,1)S(1)} %get-tuple-element.50.own_ref), channel_id=1, source_target_pairs={{0,16},{16,0},{1,17},{17,1},{2,18},{18,2},{3,19},{19,3},{4,20},{20... | collective-permute-start | bytes 589832 | tf_op jit(solution)/shard_map/ppermute | solution.py:74
  44.0 7.8 %collective-permute-start.17 = (bf16[64,2048]{1,0:T(8,128)(2,1)S(1)}, bf16[64,2048]{1,0:T(8,128)(2,1)S(1)}, u32[]{:S(2)}, u32[]{:S(2)}) collective-permute-start(bf16[64,2048]{1,0:T(8,128)(2,1)S(1)} %get-tuple-element.58), channel_id=1, source_target_pairs={{0,8},{4,12},{8,0},{12,4},{1,9},{5,13},{9,1},{13,5},{2,10},{6,14},... | collective-permute-start | bytes 786440 | tf_op jit(solution)/shard_map/ppermute | solution.py:74
  48.1 7.3 %collective-permute-start.19 = (bf16[32,2048]{1,0:T(8,128)(2,1)S(1)}, bf16[32,2048]{1,0:T(8,128)(2,1)S(1)}, u32[]{:S(2)}, u32[]{:S(2)}) collective-permute-start(bf16[32,2048]{1,0:T(8,128)(2,1)S(1)} %get-tuple-element.59), channel_id=1, source_target_pairs={{0,16},{16,0},{1,17},{17,1},{2,18},{18,2},{3,19},{19,3},{4,20},{20... | collective-permute-start | bytes 393224 | tf_op jit(solution)/shard_map/ppermute | solution.py:74
  49.6 7.9 %collective-permute-start.20 = (bf16[32,2048]{1,0:T(8,128)(2,1)S(1)}, bf16[32,2048]{1,0:T(8,128)(2,1)S(1)}, u32[]{:S(2)}, u32[]{:S(2)}) collective-permute-start(bf16[32,2048]{1,0:T(8,128)(2,1)S(1)} %get-tuple-element.60), channel_id=1, source_target_pairs={{0,24},{4,28},{8,16},{12,20},{16,8},{20,12},{24,0},{28,4},{1,25},{... | collective-permute-start | bytes 393224 | tf_op jit(solution)/shard_map/ppermute | solution.py:74
  51.9 6.1 %collective-permute-start.21 = (bf16[32,2048]{1,0:T(8,128)(2,1)S(1)}, bf16[32,2048]{1,0:T(8,128)(2,1)S(1)}, u32[]{:S(2)}, u32[]{:S(2)}) collective-permute-start(bf16[32,2048]{1,0:T(8,128)(2,1)S(1)} %get-tuple-element.61), channel_id=1, source_target_pairs={{0,17},{1,16},{2,19},{3,18},{16,1},{17,0},{18,3},{19,2},{4,21},{5,... | collective-permute-start | bytes 393224 | tf_op jit(solution)/shard_map/ppermute | solution.py:74
  55.1 5.0 %collective-permute-start.15 = (bf16[32,2048]{1,0:T(8,128)(2,1)S(1)}, bf16[32,2048]{1,0:T(8,128)(2,1)S(1)}, u32[]{:S(2)}, u32[]{:S(2)}) collective-permute-start(bf16[32,2048]{1,0:T(8,128)(2,1)S(1)} %get-tuple-element.54), channel_id=1, source_target_pairs={{0,8},{4,12},{8,0},{12,4},{1,9},{5,13},{9,1},{13,5},{2,10},{6,14},... | collective-permute-start | bytes 393224 | tf_op jit(solution)/shard_map/ppermute | solution.py:74
  55.1 5.6 %collective-permute-start.18 = (bf16[32,2048]{1,0:T(8,128)(2,1)S(1)}, bf16[32,2048]{1,0:T(8,128)(2,1)S(1)}, u32[]{:S(2)}, u32[]{:S(2)}) collective-permute-start(bf16[32,2048]{1,0:T(8,128)(2,1)S(1)} %get-tuple-element.62), channel_id=1, source_target_pairs={{0,1},{1,0},{2,3},{3,2},{4,5},{5,4},{6,7},{7,6},{8,9},{9,8},{10,11... | collective-permute-start | bytes 393224 | tf_op jit(solution)/shard_map/ppermute | solution.py:74
  60.7 5.9 %collective-permute-start.22 = (bf16[2,16,2048]{2,1,0:T(8,128)(2,1)S(1)}, bf16[2,16,2048]{2,1,0:T(8,128)(2,1)S(1)}, u32[]{:S(2)}, u32[]{:S(2)}) collective-permute-start(bf16[2,16,2048]{2,1,0:T(8,128)(2,1)S(1)} %fusion.5), channel_id=1, source_target_pairs={{0,2},{1,3},{2,0},{3,1},{4,6},{5,7},{6,4},{7,5},{8,10},{9,11},{10,... | collective-permute-start | bytes 393224 | tf_op jit(solution)/shard_map/ppermute | solution.py:74
where the time goes:
time: 68 us; the launch traced here: 67.4 us
  starting transfers between devices  29.3 us (43%)
  waiting for transfers between devices  21.8 us (32%)
  Pallas kernels  11.4 us (17%)
  local copies, waits for them, and re-layouts  3.84 us (6%)
  other arithmetic  0.87 us (1%)
    ppermute x14, starting transfers between devices, swap(): lax.ppermute(block, axes, [(place, place ^ mask) for place in range(size)])  18.2 us
    ppermute x14, waiting for transfers between devices, swap(): lax.ppermute(block, axes, [(place, place ^ mask) for place in range(size)])  15 us
    pallas_call x7, Pallas kernels, run(): pl.pallas_call(functools.partial(kernel, **sizes), out_shape=out_shape, i...  11.4 us
    ppermute x9, starting transfers between devices, turn(): return lax.ppermute(block, ('rep', 'node'), pairs)  11.1 us
    ppermute x9, waiting for transfers between devices, turn(): return lax.ppermute(block, ('rep', 'node'), pairs)  6.86 us
    unnamed x9, local copies, waits for them, and re-layouts  3.8 us
  transfers between devices with their start and end apart: 23, of which 15 were waited for; matrix products, arithmetic and copies ran while one was open for 0% of the time, Pallas kernels for 15%

commit v1 on v0

--- a/solution.py
+++ b/solution.py
@@ -321,6 +321,7 @@
     here, there = narrow(keep + wide(back_y)).reshape(2, 2 * row_count, -1)
     there = swap(there, ("rep", "local"), places | 1)
     here = swap(here, "local", 1)
+    along_x, across, here, there = together((along_x, across, here, there))
     own = keep_a + wide(along_y) + wide(here)
     other = wide(along_x) + wide(across) + wide(there)
     total = jnp.stack([own, other]).reshape(2, 2, row_count, -1)

time: 68 us -> 69 us (1.015)
  waiting for transfers between devices: 21.8 us -> 23.7 us
    ppermute x14, waiting for transfers between devices: 15 us -> 16.9 us  [swap(): lax.ppermute(block, axes, [(place, place ^ mask) for place in range(size)])]
  transfers between devices with their start and end apart: 23 -> 23, of which waited for: 15 -> 14; matrix products, arithmetic and copies ran while one was open for 0% -> 0% of each run, Pallas kernels for 15% -> 14%
where the time goes in v1:
time: 69 us; the launch traced here: 68.8 us
  starting transfers between devices  28.7 us (42%)
  waiting for transfers between devices  23.7 us (34%)
  Pallas kernels  11.4 us (17%)
  local copies, waits for them, and re-layouts  3.84 us (6%)
  other arithmetic  0.87 us (1%)
    ppermute x14, starting transfers between devices, swap(): lax.ppermute(block, axes, [(place, place ^ mask) for place in range(size)])  17.7 us
    ppermute x14, waiting for transfers between devices, swap(): lax.ppermute(block, axes, [(place, place ^ mask) for place in range(size)])  16.9 us
    pallas_call x7, Pallas kernels, run(): pl.pallas_call(functools.partial(kernel, **sizes), out_shape=out_shape, i...  11.4 us
    ppermute x9, starting transfers between devices, turn(): return lax.ppermute(block, ('rep', 'node'), pairs)  11.1 us
    ppermute x9, waiting for transfers between devices, turn(): return lax.ppermute(block, ('rep', 'node'), pairs)  6.86 us
    unnamed x9, local copies, waits for them, and re-layouts  3.8 us
  transfers between devices with their start and end apart: 23, of which 14 were waited for; matrix products, arithmetic and copies ran while one was open for 0% of the time, Pallas kernels for 14%

profile of v1, /device:TPU:0, one launch (start us, length us, event | category | flops | bytes accessed | tf_op | source)
XLA Modules:
  0.0 68.8 jit_solution(13140727033870326020)
XLA Ops:
  0.0 1.6 %shard_map.64.refs_0_ = bf16[16,4224]{1,0:T(8,128)(2,1)} custom-call(bf16[16,4096]{1,0:T(8,128)(2,1)} %tokens_in.1, s32[8,16]{1,0:T(8,128)} %bitcast.30, f32[8,16]{1,0:T(8,128)} %bitcast.31), custom_call_target="tpu_custom_call" | custom-call | bytes 132096 | tf_op jit(solution)/shard_map/pallas_call | solution.py:201
  1.6 3.0 %collective-permute-start.2 = (bf16[16,4224]{1,0:T(8,128)(2,1)}, bf16[16,4224]{1,0:T(8,128)(2,1)S(1)}, u32[]{:S(2)}, u32[]{:S(2)}) collective-permute-start(bf16[16,4224]{1,0:T(8,128)(2,1)} %shard_map.64.refs_0_), channel_id=1, source_target_pairs={{0,8},{4,20},{8,0},{12,28},{16,24},{20,4},{24,16},{28,12},{1,9},{5... | collective-permute-start | bytes 405512 | tf_op jit(solution)/shard_map/ppermute | solution.py:81
  4.6 3.6 %collective-permute-start = (bf16[16,4224]{1,0:T(8,128)(2,1)}, bf16[16,4224]{1,0:T(8,128)(2,1)S(1)}, u32[]{:S(2)}, u32[]{:S(2)}) collective-permute-start(bf16[16,4224]{1,0:T(8,128)(2,1)} %shard_map.64.refs_0_), channel_id=1, source_target_pairs={{0,3},{1,2},{2,1},{3,0},{4,7},{5,6},{6,5},{7,4},{8,11},{9,10},{10,... | collective-permute-start | bytes 405512 | tf_op jit(solution)/shard_map/ppermute | solution.py:74
  8.2 1.5 %collective-permute-start.4 = (bf16[16,4224]{1,0:T(8,128)(2,1)}, bf16[16,4224]{1,0:T(8,128)(2,1)S(1)}, u32[]{:S(2)}, u32[]{:S(2)}) collective-permute-start(bf16[16,4224]{1,0:T(8,128)(2,1)} %shard_map.64.refs_0_), channel_id=1, source_target_pairs={{0,16},{4,12},{8,24},{12,4},{16,0},{20,28},{24,8},{28,20},{1,17},{... | collective-permute-start | bytes 405512 | tf_op jit(solution)/shard_map/ppermute | solution.py:81
  9.7 0.5 collective-permute-start.3
  10.3 1.9 %copy-done.1 = bf16[1,384,4096]{2,1,0:T(8,128)(2,1)S(1)} copy-done((bf16[1,384,4096]{2,1,0:T(8,128)(2,1)S(1)}, bf16[1,384,4096]{2,1,0:T(8,128)(2,1)}, u32[]{:S(2)}) %copy-start.1) | copy-done | bytes 3145752
  12.2 1.9 %copy-done.2 = bf16[1,384,4096]{2,1,0:T(8,128)(2,1)S(1)} copy-done((bf16[1,384,4096]{2,1,0:T(8,128)(2,1)S(1)}, bf16[1,384,4096]{2,1,0:T(8,128)(2,1)}, u32[]{:S(2)}) %copy-start.2) | copy-done | bytes 3145752
  14.0 0.4 shard_map.65.refs_8_
  14.5 0.0 collective-permute-done
  14.5 0.2 collective-permute-done.1
  14.7 0.0 collective-permute-done.4.refs_4_
  14.7 0.2 collective-permute-done.3.refs_6_
  14.9 0.0 collective-permute-start.9
  14.9 1.5 %collective-permute-start.6 = (bf16[32,4224]{1,0:T(8,128)(2,1)S(1)}, bf16[32,4224]{1,0:T(8,128)(2,1)S(1)}, u32[]{:S(2)}, u32[]{:S(2)}) collective-permute-start(bf16[32,4224]{1,0:T(8,128)(2,1)S(1)} %constant_dynamic-update-slice_fusion.refs_0_.refs_1_), channel_id=1, source_target_pairs={{0,8},{4,20},{8,0},{12,28},{16,24},{20,4},{24,16},{28,12},{1,9},{5... | collective-permute-start | bytes 811016 | tf_op jit(solution)/shard_map/ppermute | solution.py:81
  16.4 0.6 collective-permute-start.7
  17.0 2.0 %collective-permute-start.5 = (bf16[16,4224]{1,0:T(8,128)(2,1)S(1)}, bf16[16,4224]{1,0:T(8,128)(2,1)S(1)}, u32[]{:S(2)}, u32[]{:S(2)}) collective-permute-start(bf16[16,4224]{1,0:T(8,128)(2,1)S(1)} %collective-permute-done), channel_id=1, source_target_pairs={{0,1},{1,0},{2,3},{3,2},{4,5},{5,4},{6,7},{7,6},{8,9},{9,8},{10,11... | collective-permute-start | bytes 405512 | tf_op jit(solution)/shard_map/ppermute | solution.py:74
  19.0 0.2 shard_map.66.down_own
  19.3 3.5 %collective-permute-done.5.refs_1_ = bf16[16,4224]{1,0:T(8,128)(2,1)S(1)} collective-permute-done((bf16[16,4224]{1,0:T(8,128)(2,1)S(1)}, bf16[16,4224]{1,0:T(8,128)(2,1)S(1)}, u32[]{:S(2)}, u32[]{:S(2)}) %collective-permute-start.5) | collective-permute-done | bytes 135200 | tf_op jit(solution)/shard_map/ppermute | solution.py:74
  22.7 0.9 %collective-permute-done.6.refs_2_.refs_3_ = bf16[32,4224]{1,0:T(8,128)(2,1)S(1)} collective-permute-done((bf16[32,4224]{1,0:T(8,128)(2,1)S(1)}, bf16[32,4224]{1,0:T(8,128)(2,1)S(1)}, u32[]{:S(2)}, u32[]{:S(2)}) %collective-permute-start.6) | collective-permute-done | bytes 270368 | tf_op jit(solution)/shard_map/ppermute | solution.py:81
  23.6 0.2 collective-permute-done.7.refs_4_.refs_5_
  23.9 0.3 collective-permute-start.13
  24.2 1.5 %collective-permute-start.8 = (bf16[32,4224]{1,0:T(8,128)(2,1)S(1)}, bf16[32,4224]{1,0:T(8,128)(2,1)S(1)}, u32[]{:S(2)}, u32[]{:S(2)}) collective-permute-start(bf16[32,4224]{1,0:T(8,128)(2,1)S(1)} %collective-permute-done.6.refs_2_.refs_3_), channel_id=1, source_target_pairs={{0,16},{4,12},{8,24},{12,4},{16,0},{20,28},{24,8},{28,20},{1,17},{... | collective-permute-start | bytes 811016 | tf_op jit(solution)/shard_map/ppermute | solution.py:81
  25.7 0.5 collective-permute-start.10
  26.2 1.5 %collective-permute-start.12 = (bf16[16,4224]{1,0:T(8,128)(2,1)S(1)}, bf16[16,4224]{1,0:T(8,128)(2,1)S(1)}, u32[]{:S(2)}, u32[]{:S(2)}) collective-permute-start(bf16[16,4224]{1,0:T(8,128)(2,1)S(1)} %collective-permute-done.5.refs_1_), channel_id=1, source_target_pairs={{0,16},{4,12},{8,24},{12,4},{16,0},{20,28},{24,8},{28,20},{1,17},{... | collective-permute-start | bytes 405512 | tf_op jit(solution)/shard_map/ppermute | solution.py:81
  27.6 4.5 %collective-permute-done.10.refs_3_ = bf16[16,4224]{1,0:T(8,128)(2,1)S(1)} collective-permute-done((bf16[16,4224]{1,0:T(8,128)(2,1)S(1)}, bf16[16,4224]{1,0:T(8,128)(2,1)S(1)}, u32[]{:S(2)}, u32[]{:S(2)}) %collective-permute-start.10) | collective-permute-done | bytes 135200 | tf_op jit(solution)/shard_map/ppermute | solution.py:81
  32.2 0.5 collective-permute-start.11
  32.7 3.5 %shard_map.67 = (bf16[2,128,384]{2,1,0:T(8,128)(2,1)S(1)}, f32[2,128,128]{2,1,0:T(8,128)S(1)}) custom-call(bf16[32,4224]{1,0:T(8,128)(2,1)S(1)} %constant_dynamic-update-slice_fusion.refs_0_.refs_1_, bf16[32,4224]{1,0:T(8,128)(2,1)S(1)} %constant_dynamic-update-slice_fusion.refs_0_.refs_1_, bf16[32,4224]{1,0:T(8,128)(2,1)S(1)} %collective-permute-done.6.refs_2_.refs_3_, ...), custom_call_target="tpu_custom_call" | custom-call | flops 1610612736 | bytes 14745600 | tf_op jit(solution)/shard_map/pallas_call | solution.py:201
  36.2 1.0 %collective-permute-done.11.refs_7_ = bf16[16,4224]{1,0:T(8,128)(2,1)S(1)} collective-permute-done((bf16[16,4224]{1,0:T(8,128)(2,1)S(1)}, bf16[16,4224]{1,0:T(8,128)(2,1)S(1)}, u32[]{:S(2)}, u32[]{:S(2)}) %collective-permute-start.11) | collective-permute-done | bytes 135200 | tf_op jit(solution)/shard_map/ppermute | solution.py:81
  37.2 0.6 collective-permute-start.18
  37.8 3.5 %shard_map.68 = (bf16[2,128,384]{2,1,0:T(8,128)(2,1)S(1)}, f32[2,128,128]{2,1,0:T(8,128)S(1)}) custom-call(bf16[16,4224]{1,0:T(8,128)(2,1)S(1)} %copy-done.3, bf16[16,4224]{1,0:T(8,128)(2,1)S(1)} %collective-permute-done.5.refs_1_, bf16[16,4224]{1,0:T(8,128)(2,1)S(1)} %collective-permute-done.2.refs_2_, ...), custom_call_target="tpu_custom_call" | custom-call | flops 1610612736 | bytes 13664256 | tf_op jit(solution)/shard_map/pallas_call | solution.py:201
  41.3 1.5 %collective-permute-start.14 = (bf16[2,128,384]{2,1,0:T(8,128)(2,1)S(1)}, bf16[2,128,384]{2,1,0:T(8,128)(2,1)S(1)}, u32[]{:S(2)}, u32[]{:S(2)}) collective-permute-start(bf16[2,128,384]{2,1,0:T(8,128)(2,1)S(1)} %get-tuple-element.54.own_ref), channel_id=1, source_target_pairs={{0,16},{16,0},{1,17},{17,1},{2,18},{18,2},{3,19},{19,3},{4,20},{20... | collective-permute-start | bytes 589832 | tf_op jit(solution)/shard_map/ppermute | solution.py:74
  42.8 0.1 collective-permute-done.18.other_ref
  42.9 1.1 %shard_map.70 = (f32[64,2048]{1,0:T(8,128)S(1)}, bf16[64,2048]{1,0:T(8,128)(2,1)S(1)}) custom-call(bf16[2,128,384]{2,1,0:T(8,128)(2,1)S(1)} %get-tuple-element.61.own_ref, bf16[2,128,384]{2,1,0:T(8,128)(2,1)S(1)} %collective-permute-done.18.other_ref, f32[2,128,128]{2,1,0:T(8,128)S(1)} %get-tuple-element.62.share_ref, ...), custom_call_target="tpu_custom_call" | custom-call | flops 805306368 | bytes 6815744 | tf_op jit(solution)/shard_map/pallas_call | solution.py:201
  44.0 1.1 %collective-permute-start.19 = (bf16[64,2048]{1,0:T(8,128)(2,1)S(1)}, bf16[64,2048]{1,0:T(8,128)(2,1)S(1)}, u32[]{:S(2)}, u32[]{:S(2)}) collective-permute-start(bf16[64,2048]{1,0:T(8,128)(2,1)S(1)} %get-tuple-element.64), channel_id=1, source_target_pairs={{0,8},{4,12},{8,0},{12,4},{1,9},{5,13},{9,1},{13,5},{2,10},{6,14},... | collective-permute-start | bytes 786440 | tf_op jit(solution)/shard_map/ppermute | solution.py:74
  45.1 2.0 %collective-permute-done.14.other_ref = bf16[2,128,384]{2,1,0:T(8,128)(2,1)S(1)} collective-permute-done((bf16[2,128,384]{2,1,0:T(8,128)(2,1)S(1)}, bf16[2,128,384]{2,1,0:T(8,128)(2,1)S(1)}, u32[]{:S(2)}, u32[]{:S(2)}) %collective-permute-start.14) | collective-permute-done | bytes 196640 | tf_op jit(solution)/shard_map/ppermute | solution.py:74
  47.1 1.1 %shard_map.69 = (f32[32,2048]{1,0:T(8,128)S(1)}, bf16[32,2048]{1,0:T(8,128)(2,1)S(1)}, bf16[32,2048]{1,0:T(8,128)(2,1)S(1)}, bf16[32,2048]{1,0:T(8,128)(2,1)S(1)}) custom-call(bf16[2,128,384]{2,1,0:T(8,128)(2,1)S(1)} %get-tuple-element.54.own_ref, bf16[2,128,384]{2,1,0:T(8,128)(2,1)S(1)} %collective-permute-done.14.other_ref, ...), custom_call_target="tpu_custom_call" | custom-call | flops 805306368 | bytes 6815744 | tf_op jit(solution)/shard_map/pallas_call | solution.py:201
  48.1 1.5 %collective-permute-start.16 = (bf16[32,2048]{1,0:T(8,128)(2,1)S(1)}, bf16[32,2048]{1,0:T(8,128)(2,1)S(1)}, u32[]{:S(2)}, u32[]{:S(2)}) collective-permute-start(bf16[32,2048]{1,0:T(8,128)(2,1)S(1)} %get-tuple-element.59), channel_id=1, source_target_pairs={{0,16},{16,0},{1,17},{17,1},{2,18},{18,2},{3,19},{19,3},{4,20},{20... | collective-permute-start | bytes 393224 | tf_op jit(solution)/shard_map/ppermute | solution.py:74
  49.6 1.4 %collective-permute-start.17 = (bf16[32,2048]{1,0:T(8,128)(2,1)S(1)}, bf16[32,2048]{1,0:T(8,128)(2,1)S(1)}, u32[]{:S(2)}, u32[]{:S(2)}) collective-permute-start(bf16[32,2048]{1,0:T(8,128)(2,1)S(1)} %get-tuple-element.60), channel_id=1, source_target_pairs={{0,24},{4,28},{8,16},{12,20},{16,8},{20,12},{24,0},{28,4},{1,25},{... | collective-permute-start | bytes 393224 | tf_op jit(solution)/shard_map/ppermute | solution.py:74
  51.0 0.8 %collective-permute-done.19 = bf16[64,2048]{1,0:T(8,128)(2,1)S(1)} collective-permute-done((bf16[64,2048]{1,0:T(8,128)(2,1)S(1)}, bf16[64,2048]{1,0:T(8,128)(2,1)S(1)}, u32[]{:S(2)}, u32[]{:S(2)}) %collective-permute-start.19) | collective-permute-done | bytes 262176 | tf_op jit(solution)/shard_map/ppermute | solution.py:74
  51.9 2.1 %collective-permute-start.20 = (bf16[32,2048]{1,0:T(8,128)(2,1)S(1)}, bf16[32,2048]{1,0:T(8,128)(2,1)S(1)}, u32[]{:S(2)}, u32[]{:S(2)}) collective-permute-start(bf16[32,2048]{1,0:T(8,128)(2,1)S(1)} %get-tuple-element.70), channel_id=1, source_target_pairs={{0,1},{1,0},{2,3},{3,2},{4,5},{5,4},{6,7},{7,6},{8,9},{9,8},{10,11... | collective-permute-start | bytes 393224 | tf_op jit(solution)/shard_map/ppermute | solution.py:74
  54.0 0.7 %collective-permute-start.21 = (bf16[32,2048]{1,0:T(8,128)(2,1)S(1)}, bf16[32,2048]{1,0:T(8,128)(2,1)S(1)}, u32[]{:S(2)}, u32[]{:S(2)}) collective-permute-start(bf16[32,2048]{1,0:T(8,128)(2,1)S(1)} %get-tuple-element.69), channel_id=1, source_target_pairs={{0,17},{1,16},{2,19},{3,18},{16,1},{17,0},{18,3},{19,2},{4,21},{5,... | collective-permute-start | bytes 393224 | tf_op jit(solution)/shard_map/ppermute | solution.py:74
  54.8 0.7 collective-permute-start.15
  55.4 1.3 %collective-permute-done.17 = bf16[32,2048]{1,0:T(8,128)(2,1)S(1)} collective-permute-done((bf16[32,2048]{1,0:T(8,128)(2,1)S(1)}, bf16[32,2048]{1,0:T(8,128)(2,1)S(1)}, u32[]{:S(2)}, u32[]{:S(2)}) %collective-permute-start.17) | collective-permute-done | bytes 131104 | tf_op jit(solution)/shard_map/ppermute | solution.py:74
  56.8 0.2 collective-permute-done.20
  57.0 3.5 %collective-permute-done.21 = bf16[32,2048]{1,0:T(8,128)(2,1)S(1)} collective-permute-done((bf16[32,2048]{1,0:T(8,128)(2,1)S(1)}, bf16[32,2048]{1,0:T(8,128)(2,1)S(1)}, u32[]{:S(2)}, u32[]{:S(2)}) %collective-permute-start.21) | collective-permute-done | bytes 131104 | tf_op jit(solution)/shard_map/ppermute | solution.py:74
  60.7 2.1 %collective-permute-start.22 = (bf16[2,16,2048]{2,1,0:T(8,128)(2,1)S(1)}, bf16[2,16,2048]{2,1,0:T(8,128)(2,1)S(1)}, u32[]{:S(2)}, u32[]{:S(2)}) collective-permute-start(bf16[2,16,2048]{2,1,0:T(8,128)(2,1)S(1)} %fusion.5), channel_id=1, source_target_pairs={{0,2},{1,3},{2,0},{3,1},{4,6},{5,7},{6,4},{7,5},{8,10},{9,11},{10,... | collective-permute-start | bytes 393224 | tf_op jit(solution)/shard_map/ppermute | solution.py:74
  62.8 5.2 %collective-permute-done.22 = bf16[2,16,2048]{2,1,0:T(8,128)(2,1)S(1)} collective-permute-done((bf16[2,16,2048]{2,1,0:T(8,128)(2,1)S(1)}, bf16[2,16,2048]{2,1,0:T(8,128)(2,1)S(1)}, u32[]{:S(2)}, u32[]{:S(2)}) %collective-permute-start.22) | collective-permute-done | bytes 131104 | tf_op jit(solution)/shard_map/ppermute | solution.py:74
  68.1 0.7 %maximum_select_fusion = bf16[16,4096]{1,0:T(8,128)(2,1)} fusion(bf16[16,2048]{1,0:T(8,128)(2,1)S(1)} %get-tuple-element.72, bf16[16,2048]{1,0:T(8,128)(2,1)S(1)} %get-tuple-element.71, pred[]{:T(512)S(6)} %eq.3), kind=kLoop, calls=%fused_computation.12 | loop fusion | flops 589824 | bytes 262145 | tf_op jit(solution)/shard_map/jit(_where)/select_n | solution.py:329
  (23 shorter events, 0.3 us)
Async XLA Ops:
  1.6 8.1 %collective-permute-start.2 = (bf16[16,4224]{1,0:T(8,128)(2,1)}, bf16[16,4224]{1,0:T(8,128)(2,1)S(1)}, u32[]{:S(2)}, u32[]{:S(2)}) collective-permute-start(bf16[16,4224]{1,0:T(8,128)(2,1)} %shard_map.64.refs_0_), channel_id=1, source_target_pairs={{0,8},{4,20},{8,0},{12,28},{16,24},{20,4},{24,16},{28,12},{1,9},{5... | collective-permute-start | bytes 405512 | tf_op jit(solution)/shard_map/ppermute | solution.py:81
  4.6 9.9 %collective-permute-start = (bf16[16,4224]{1,0:T(8,128)(2,1)}, bf16[16,4224]{1,0:T(8,128)(2,1)S(1)}, u32[]{:S(2)}, u32[]{:S(2)}) collective-permute-start(bf16[16,4224]{1,0:T(8,128)(2,1)} %shard_map.64.refs_0_), channel_id=1, source_target_pairs={{0,3},{1,2},{2,1},{3,0},{4,7},{5,6},{6,5},{7,4},{8,11},{9,10},{10,... | collective-permute-start | bytes 405512 | tf_op jit(solution)/shard_map/ppermute | solution.py:74
  8.2 6.5 %collective-permute-start.1 = (bf16[16,4224]{1,0:T(8,128)(2,1)}, bf16[16,4224]{1,0:T(8,128)(2,1)S(1)}, u32[]{:S(2)}, u32[]{:S(2)}) collective-permute-start(bf16[16,4224]{1,0:T(8,128)(2,1)} %shard_map.64.refs_0_), channel_id=1, source_target_pairs={{0,1},{1,0},{2,3},{3,2},{4,5},{5,4},{6,7},{7,6},{8,9},{9,8},{10,11... | collective-permute-start | bytes 405512 | tf_op jit(solution)/shard_map/ppermute | solution.py:74
  8.2 6.5 %collective-permute-start.4 = (bf16[16,4224]{1,0:T(8,128)(2,1)}, bf16[16,4224]{1,0:T(8,128)(2,1)S(1)}, u32[]{:S(2)}, u32[]{:S(2)}) collective-permute-start(bf16[16,4224]{1,0:T(8,128)(2,1)} %shard_map.64.refs_0_), channel_id=1, source_target_pairs={{0,16},{4,12},{8,24},{12,4},{16,0},{20,28},{24,8},{28,20},{1,17},{... | collective-permute-start | bytes 405512 | tf_op jit(solution)/shard_map/ppermute | solution.py:81
  9.7 5.2 %collective-permute-start.3 = (bf16[16,4224]{1,0:T(8,128)(2,1)S(1)}, bf16[16,4224]{1,0:T(8,128)(2,1)S(1)}, u32[]{:S(2)}, u32[]{:S(2)}) collective-permute-start(bf16[16,4224]{1,0:T(8,128)(2,1)S(1)} %collective-permute-done.2.refs_2_), channel_id=1, source_target_pairs={{0,16},{4,12},{8,24},{12,4},{16,0},{20,28},{24,8},{28,20},{1,17},{... | collective-permute-start | bytes 405512 | tf_op jit(solution)/shard_map/ppermute | solution.py:81
  10.3 1.9 %copy-start.1 = (bf16[1,384,4096]{2,1,0:T(8,128)(2,1)S(1)}, bf16[1,384,4096]{2,1,0:T(8,128)(2,1)}, u32[]{:S(2)}) copy-start(bf16[1,384,4096]{2,1,0:T(8,128)(2,1)} %param.9) | copy-start | bytes 9437188
  12.1 1.9 %copy-start.2 = (bf16[1,384,4096]{2,1,0:T(8,128)(2,1)S(1)}, bf16[1,384,4096]{2,1,0:T(8,128)(2,1)}, u32[]{:S(2)}) copy-start(bf16[1,384,4096]{2,1,0:T(8,128)(2,1)} %param.10) | copy-start | bytes 9437188
  14.0 5.0 %copy-start = (bf16[1,768,2048]{2,1,0:T(8,128)(2,1)S(1)}, bf16[1,768,2048]{2,1,0:T(8,128)(2,1)}, u32[]{:S(2)}) copy-start(bf16[1,768,2048]{2,1,0:T(8,128)(2,1)} %param.11) | copy-start | bytes 9437188
  14.9 17.8 %collective-permute-start.9 = (bf16[768,4096]{1,0:T(8,128)(2,1)S(1)}, bf16[768,4096]{1,0:T(8,128)(2,1)S(1)}, u32[]{:S(2)}, u32[]{:S(2)}) collective-permute-start(bf16[768,4096]{1,0:T(8,128)(2,1)S(1)} %shard_map.65.refs_8_), channel_id=1, source_target_pairs={{0,4},{4,0},{8,12},{12,8},{1,5},{5,1},{9,13},{13,9},{2,6},{6,2},{1... | collective-permute-start | bytes 18874376 | tf_op jit(solution)/shard_map/ppermute | solution.py:74
  14.9 8.7 %collective-permute-start.6 = (bf16[32,4224]{1,0:T(8,128)(2,1)S(1)}, bf16[32,4224]{1,0:T(8,128)(2,1)S(1)}, u32[]{:S(2)}, u32[]{:S(2)}) collective-permute-start(bf16[32,4224]{1,0:T(8,128)(2,1)S(1)} %constant_dynamic-update-slice_fusion.refs_0_.refs_1_), channel_id=1, source_target_pairs={{0,8},{4,20},{8,0},{12,28},{16,24},{20,4},{24,16},{28,12},{1,9},{5... | collective-permute-start | bytes 811016 | tf_op jit(solution)/shard_map/ppermute | solution.py:81
  16.4 7.5 %collective-permute-start.7 = (bf16[32,4224]{1,0:T(8,128)(2,1)S(1)}, bf16[32,4224]{1,0:T(8,128)(2,1)S(1)}, u32[]{:S(2)}, u32[]{:S(2)}) collective-permute-start(bf16[32,4224]{1,0:T(8,128)(2,1)S(1)} %constant_dynamic-update-slice_fusion.refs_0_.refs_1_), channel_id=1, source_target_pairs={{0,16},{4,12},{8,24},{12,4},{16,0},{20,28},{24,8},{28,20},{1,17},{... | collective-permute-start | bytes 811016 | tf_op jit(solution)/shard_map/ppermute | solution.py:81
  17.0 5.7 %collective-permute-start.5 = (bf16[16,4224]{1,0:T(8,128)(2,1)S(1)}, bf16[16,4224]{1,0:T(8,128)(2,1)S(1)}, u32[]{:S(2)}, u32[]{:S(2)}) collective-permute-start(bf16[16,4224]{1,0:T(8,128)(2,1)S(1)} %collective-permute-done), channel_id=1, source_target_pairs={{0,1},{1,0},{2,3},{3,2},{4,5},{5,4},{6,7},{7,6},{8,9},{9,8},{10,11... | collective-permute-start | bytes 405512 | tf_op jit(solution)/shard_map/ppermute | solution.py:74
  19.3 18.6 %copy-start.3 = (bf16[16,4224]{1,0:T(8,128)(2,1)S(1)}, bf16[16,4224]{1,0:T(8,128)(2,1)}, u32[]{:S(2)}) copy-start(bf16[16,4224]{1,0:T(8,128)(2,1)} %shard_map.64.refs_0_) | copy-start | bytes 405508
  23.9 13.3 %collective-permute-start.13 = (bf16[768,2048]{1,0:T(8,128)(2,1)S(1)}, bf16[768,2048]{1,0:T(8,128)(2,1)S(1)}, u32[]{:S(2)}, u32[]{:S(2)}) collective-permute-start(bf16[768,2048]{1,0:T(8,128)(2,1)S(1)} %shard_map.66.down_own), channel_id=1, source_target_pairs={{0,4},{4,0},{8,12},{12,8},{1,5},{5,1},{9,13},{13,9},{2,6},{6,2},{1... | collective-permute-start | bytes 9437192 | tf_op jit(solution)/shard_map/ppermute | solution.py:74
  24.2 8.5 %collective-permute-start.8 = (bf16[32,4224]{1,0:T(8,128)(2,1)S(1)}, bf16[32,4224]{1,0:T(8,128)(2,1)S(1)}, u32[]{:S(2)}, u32[]{:S(2)}) collective-permute-start(bf16[32,4224]{1,0:T(8,128)(2,1)S(1)} %collective-permute-done.6.refs_2_.refs_3_), channel_id=1, source_target_pairs={{0,16},{4,12},{8,24},{12,4},{16,0},{20,28},{24,8},{28,20},{1,17},{... | collective-permute-start | bytes 811016 | tf_op jit(solution)/shard_map/ppermute | solution.py:81
  25.7 6.5 %collective-permute-start.10 = (bf16[16,4224]{1,0:T(8,128)(2,1)S(1)}, bf16[16,4224]{1,0:T(8,128)(2,1)S(1)}, u32[]{:S(2)}, u32[]{:S(2)}) collective-permute-start(bf16[16,4224]{1,0:T(8,128)(2,1)S(1)} %collective-permute-done.5.refs_1_), channel_id=1, source_target_pairs={{0,8},{4,20},{8,0},{12,28},{16,24},{20,4},{24,16},{28,12},{1,9},{5... | collective-permute-start | bytes 405512 | tf_op jit(solution)/shard_map/ppermute | solution.py:81
  26.2 10.0 %collective-permute-start.12 = (bf16[16,4224]{1,0:T(8,128)(2,1)S(1)}, bf16[16,4224]{1,0:T(8,128)(2,1)S(1)}, u32[]{:S(2)}, u32[]{:S(2)}) collective-permute-start(bf16[16,4224]{1,0:T(8,128)(2,1)S(1)} %collective-permute-done.5.refs_1_), channel_id=1, source_target_pairs={{0,16},{4,12},{8,24},{12,4},{16,0},{20,28},{24,8},{28,20},{1,17},{... | collective-permute-start | bytes 405512 | tf_op jit(solution)/shard_map/ppermute | solution.py:81
  32.2 5.0 %collective-permute-start.11 = (bf16[16,4224]{1,0:T(8,128)(2,1)S(1)}, bf16[16,4224]{1,0:T(8,128)(2,1)S(1)}, u32[]{:S(2)}, u32[]{:S(2)}) collective-permute-start(bf16[16,4224]{1,0:T(8,128)(2,1)S(1)} %collective-permute-done.10.refs_3_), channel_id=1, source_target_pairs={{0,16},{4,12},{8,24},{12,4},{16,0},{20,28},{24,8},{28,20},{1,17},{... | collective-permute-start | bytes 405512 | tf_op jit(solution)/shard_map/ppermute | solution.py:81
  37.2 5.7 %collective-permute-start.18 = (bf16[2,128,384]{2,1,0:T(8,128)(2,1)S(1)}, bf16[2,128,384]{2,1,0:T(8,128)(2,1)S(1)}, u32[]{:S(2)}, u32[]{:S(2)}) collective-permute-start(bf16[2,128,384]{2,1,0:T(8,128)(2,1)S(1)} %get-tuple-element.61.own_ref), channel_id=1, source_target_pairs={{0,16},{16,0},{1,17},{17,1},{2,18},{18,2},{3,19},{19,3},{4,20},{20... | collective-permute-start | bytes 589832 | tf_op jit(solution)/shard_map/ppermute | solution.py:74
  41.3 5.7 %collective-permute-start.14 = (bf16[2,128,384]{2,1,0:T(8,128)(2,1)S(1)}, bf16[2,128,384]{2,1,0:T(8,128)(2,1)S(1)}, u32[]{:S(2)}, u32[]{:S(2)}) collective-permute-start(bf16[2,128,384]{2,1,0:T(8,128)(2,1)S(1)} %get-tuple-element.54.own_ref), channel_id=1, source_target_pairs={{0,16},{16,0},{1,17},{17,1},{2,18},{18,2},{3,19},{19,3},{4,20},{20... | collective-permute-start | bytes 589832 | tf_op jit(solution)/shard_map/ppermute | solution.py:74
  44.0 7.8 %collective-permute-start.19 = (bf16[64,2048]{1,0:T(8,128)(2,1)S(1)}, bf16[64,2048]{1,0:T(8,128)(2,1)S(1)}, u32[]{:S(2)}, u32[]{:S(2)}) collective-permute-start(bf16[64,2048]{1,0:T(8,128)(2,1)S(1)} %get-tuple-element.64), channel_id=1, source_target_pairs={{0,8},{4,12},{8,0},{12,4},{1,9},{5,13},{9,1},{13,5},{2,10},{6,14},... | collective-permute-start | bytes 786440 | tf_op jit(solution)/shard_map/ppermute | solution.py:74
  48.1 7.3 %collective-permute-start.16 = (bf16[32,2048]{1,0:T(8,128)(2,1)S(1)}, bf16[32,2048]{1,0:T(8,128)(2,1)S(1)}, u32[]{:S(2)}, u32[]{:S(2)}) collective-permute-start(bf16[32,2048]{1,0:T(8,128)(2,1)S(1)} %get-tuple-element.59), channel_id=1, source_target_pairs={{0,16},{16,0},{1,17},{17,1},{2,18},{18,2},{3,19},{19,3},{4,20},{20... | collective-permute-start | bytes 393224 | tf_op jit(solution)/shard_map/ppermute | solution.py:74
  49.6 7.2 %collective-permute-start.17 = (bf16[32,2048]{1,0:T(8,128)(2,1)S(1)}, bf16[32,2048]{1,0:T(8,128)(2,1)S(1)}, u32[]{:S(2)}, u32[]{:S(2)}) collective-permute-start(bf16[32,2048]{1,0:T(8,128)(2,1)S(1)} %get-tuple-element.60), channel_id=1, source_target_pairs={{0,24},{4,28},{8,16},{12,20},{16,8},{20,12},{24,0},{28,4},{1,25},{... | collective-permute-start | bytes 393224 | tf_op jit(solution)/shard_map/ppermute | solution.py:74
  51.9 5.1 %collective-permute-start.20 = (bf16[32,2048]{1,0:T(8,128)(2,1)S(1)}, bf16[32,2048]{1,0:T(8,128)(2,1)S(1)}, u32[]{:S(2)}, u32[]{:S(2)}) collective-permute-start(bf16[32,2048]{1,0:T(8,128)(2,1)S(1)} %get-tuple-element.70), channel_id=1, source_target_pairs={{0,1},{1,0},{2,3},{3,2},{4,5},{5,4},{6,7},{7,6},{8,9},{9,8},{10,11... | collective-permute-start | bytes 393224 | tf_op jit(solution)/shard_map/ppermute | solution.py:74
  54.0 6.5 %collective-permute-start.21 = (bf16[32,2048]{1,0:T(8,128)(2,1)S(1)}, bf16[32,2048]{1,0:T(8,128)(2,1)S(1)}, u32[]{:S(2)}, u32[]{:S(2)}) collective-permute-start(bf16[32,2048]{1,0:T(8,128)(2,1)S(1)} %get-tuple-element.69), channel_id=1, source_target_pairs={{0,17},{1,16},{2,19},{3,18},{16,1},{17,0},{18,3},{19,2},{4,21},{5,... | collective-permute-start | bytes 393224 | tf_op jit(solution)/shard_map/ppermute | solution.py:74
  54.8 5.8 %collective-permute-start.15 = (bf16[32,2048]{1,0:T(8,128)(2,1)S(1)}, bf16[32,2048]{1,0:T(8,128)(2,1)S(1)}, u32[]{:S(2)}, u32[]{:S(2)}) collective-permute-start(bf16[32,2048]{1,0:T(8,128)(2,1)S(1)} %get-tuple-element.58), channel_id=1, source_target_pairs={{0,8},{4,12},{8,0},{12,4},{1,9},{5,13},{9,1},{13,5},{2,10},{6,14},... | collective-permute-start | bytes 393224 | tf_op jit(solution)/shard_map/ppermute | solution.py:74
  60.7 7.3 %collective-permute-start.22 = (bf16[2,16,2048]{2,1,0:T(8,128)(2,1)S(1)}, bf16[2,16,2048]{2,1,0:T(8,128)(2,1)S(1)}, u32[]{:S(2)}, u32[]{:S(2)}) collective-permute-start(bf16[2,16,2048]{2,1,0:T(8,128)(2,1)S(1)} %fusion.5), channel_id=1, source_target_pairs={{0,2},{1,3},{2,0},{3,1},{4,6},{5,7},{6,4},{7,5},{8,10},{9,11},{10,... | collective-permute-start | bytes 393224 | tf_op jit(solution)/shard_map/ppermute | solution.py:74

commit v2 on v0

--- a/solution.py
+++ b/solution.py
@@ -284,10 +284,10 @@
     together = lax.optimization_barrier
 
     packed = pack(tokens, expert_ids, route_weights, experts)
-    line_3, line_1, square_0, gates = together(
+    line_1, line_3, square_0, gates = together(
         (
+            swap(packed, "local", 1),
             swap(packed, "local", 3),
-            swap(packed, "local", 1),
             square(packed),
             fetch((gate_local, up_local)),
         )

time: 68 us -> 68.9 us (1.013)
  waiting for transfers between devices: 21.8 us -> 26.7 us
  starting transfers between devices: 29.3 us -> 25.7 us
    ppermute x14, waiting for transfers between devices: 15 us -> 19.1 us  [swap(): lax.ppermute(block, axes, [(place, place ^ mask) for place in range(size)])]
    ppermute x14, starting transfers between devices: 18.2 us -> 14.9 us  [swap(): lax.ppermute(block, axes, [(place, place ^ mask) for place in range(size)])]
    ppermute x9, waiting for transfers between devices: 6.86 us -> 7.63 us  [turn(): return lax.ppermute(block, ('rep', 'node'), pairs)]
  transfers between devices with their start and end apart: 23 -> 23, of which waited for: 15 -> 14; matrix products, arithmetic and copies ran while one was open for 0% -> 0% of each run, Pallas kernels for 15% -> 14%
where the time goes in v2:
time: 68.9 us; the launch traced here: 68.7 us
  waiting for transfers between devices  26.7 us (39%)
  starting transfers between devices  25.7 us (37%)
  Pallas kernels  11.4 us (17%)
  local copies, waits for them, and re-layouts  3.84 us (6%)
  other arithmetic  0.87 us (1%)
    ppermute x14, waiting for transfers between devices, swap(): lax.ppermute(block, axes, [(place, place ^ mask) for place in range(size)])  19.1 us
    ppermute x14, starting transfers between devices, swap(): lax.ppermute(block, axes, [(place, place ^ mask) for place in range(size)])  14.9 us
    pallas_call x7, Pallas kernels, run(): pl.pallas_call(functools.partial(kernel, **sizes), out_shape=out_shape, i...  11.4 us
    ppermute x9, starting transfers between devices, turn(): return lax.ppermute(block, ('rep', 'node'), pairs)  10.8 us
    ppermute x9, waiting for transfers between devices, turn(): return lax.ppermute(block, ('rep', 'node'), pairs)  7.63 us
    unnamed x9, local copies, waits for them, and re-layouts  3.8 us
  transfers between devices with their start and end apart: 23, of which 14 were waited for; matrix products, arithmetic and copies ran while one was open for 0% of the time, Pallas kernels for 14%

profile of v2, /device:TPU:0, one launch (start us, length us, event | category | flops | bytes accessed | tf_op | source)
XLA Modules:
  0.0 68.7 jit_solution(13160216550986233163)
XLA Ops:
  0.0 1.6 %shard_map.64.refs_0_ = bf16[16,4224]{1,0:T(8,128)(2,1)} custom-call(bf16[16,4096]{1,0:T(8,128)(2,1)} %tokens_in.1, s32[8,16]{1,0:T(8,128)} %bitcast.30, f32[8,16]{1,0:T(8,128)} %bitcast.31), custom_call_target="tpu_custom_call" | custom-call | bytes 132096 | tf_op jit(solution)/shard_map/pallas_call | solution.py:201
  1.6 3.0 %collective-permute-start.2 = (bf16[16,4224]{1,0:T(8,128)(2,1)}, bf16[16,4224]{1,0:T(8,128)(2,1)S(1)}, u32[]{:S(2)}, u32[]{:S(2)}) collective-permute-start(bf16[16,4224]{1,0:T(8,128)(2,1)} %shard_map.64.refs_0_), channel_id=1, source_target_pairs={{0,8},{4,20},{8,0},{12,28},{16,24},{20,4},{24,16},{28,12},{1,9},{5... | collective-permute-start | bytes 405512 | tf_op jit(solution)/shard_map/ppermute | solution.py:81
  4.6 1.6 %collective-permute-start = (bf16[16,4224]{1,0:T(8,128)(2,1)}, bf16[16,4224]{1,0:T(8,128)(2,1)S(1)}, u32[]{:S(2)}, u32[]{:S(2)}) collective-permute-start(bf16[16,4224]{1,0:T(8,128)(2,1)} %shard_map.64.refs_0_), channel_id=1, source_target_pairs={{0,1},{1,0},{2,3},{3,2},{4,5},{5,4},{6,7},{7,6},{8,9},{9,8},{10,11... | collective-permute-start | bytes 405512 | tf_op jit(solution)/shard_map/ppermute | solution.py:74
  6.2 2.5 %collective-permute-start.1 = (bf16[16,4224]{1,0:T(8,128)(2,1)}, bf16[16,4224]{1,0:T(8,128)(2,1)S(1)}, u32[]{:S(2)}, u32[]{:S(2)}) collective-permute-start(bf16[16,4224]{1,0:T(8,128)(2,1)} %shard_map.64.refs_0_), channel_id=1, source_target_pairs={{0,3},{1,2},{2,1},{3,0},{4,7},{5,6},{6,5},{7,4},{8,11},{9,10},{10,... | collective-permute-start | bytes 405512 | tf_op jit(solution)/shard_map/ppermute | solution.py:74
  8.7 1.5 %collective-permute-start.4 = (bf16[16,4224]{1,0:T(8,128)(2,1)}, bf16[16,4224]{1,0:T(8,128)(2,1)S(1)}, u32[]{:S(2)}, u32[]{:S(2)}) collective-permute-start(bf16[16,4224]{1,0:T(8,128)(2,1)} %shard_map.64.refs_0_), channel_id=1, source_target_pairs={{0,16},{4,12},{8,24},{12,4},{16,0},{20,28},{24,8},{28,20},{1,17},{... | collective-permute-start | bytes 405512 | tf_op jit(solution)/shard_map/ppermute | solution.py:81
  10.2 0.0 collective-permute-done.2.refs_2_
  10.2 0.5 collective-permute-start.3
  10.7 1.9 %copy-done.1 = bf16[1,384,4096]{2,1,0:T(8,128)(2,1)S(1)} copy-done((bf16[1,384,4096]{2,1,0:T(8,128)(2,1)S(1)}, bf16[1,384,4096]{2,1,0:T(8,128)(2,1)}, u32[]{:S(2)}) %copy-start.1) | copy-done | bytes 3145752
  12.6 1.9 %copy-done.2 = bf16[1,384,4096]{2,1,0:T(8,128)(2,1)S(1)} copy-done((bf16[1,384,4096]{2,1,0:T(8,128)(2,1)S(1)}, bf16[1,384,4096]{2,1,0:T(8,128)(2,1)}, u32[]{:S(2)}) %copy-start.2) | copy-done | bytes 3145752
  14.5 0.4 shard_map.65.refs_8_
  14.9 0.0 collective-permute-done.1
  15.0 0.4 collective-permute-done.3.refs_6_
  15.4 1.1 %collective-permute-start.6 = (bf16[32,4224]{1,0:T(8,128)(2,1)S(1)}, bf16[32,4224]{1,0:T(8,128)(2,1)S(1)}, u32[]{:S(2)}, u32[]{:S(2)}) collective-permute-start(bf16[32,4224]{1,0:T(8,128)(2,1)S(1)} %constant_dynamic-update-slice_fusion.refs_0_.refs_1_), channel_id=1, source_target_pairs={{0,8},{4,20},{8,0},{12,28},{16,24},{20,4},{24,16},{28,12},{1,9},{5... | collective-permute-start | bytes 811016 | tf_op jit(solution)/shard_map/ppermute | solution.py:81
  16.5 0.9 %collective-permute-start.7 = (bf16[32,4224]{1,0:T(8,128)(2,1)S(1)}, bf16[32,4224]{1,0:T(8,128)(2,1)S(1)}, u32[]{:S(2)}, u32[]{:S(2)}) collective-permute-start(bf16[32,4224]{1,0:T(8,128)(2,1)S(1)} %constant_dynamic-update-slice_fusion.refs_0_.refs_1_), channel_id=1, source_target_pairs={{0,16},{4,12},{8,24},{12,4},{16,0},{20,28},{24,8},{28,20},{1,17},{... | collective-permute-start | bytes 811016 | tf_op jit(solution)/shard_map/ppermute | solution.py:81
  17.4 0.7 collective-permute-start.5
  18.1 0.2 shard_map.66.down_own
  18.4 4.5 %collective-permute-done.5.refs_1_ = bf16[16,4224]{1,0:T(8,128)(2,1)S(1)} collective-permute-done((bf16[16,4224]{1,0:T(8,128)(2,1)S(1)}, bf16[16,4224]{1,0:T(8,128)(2,1)S(1)}, u32[]{:S(2)}, u32[]{:S(2)}) %collective-permute-start.5) | collective-permute-done | bytes 135200 | tf_op jit(solution)/shard_map/ppermute | solution.py:74
  22.9 1.2 %collective-permute-done.6.refs_2_.refs_3_ = bf16[32,4224]{1,0:T(8,128)(2,1)S(1)} collective-permute-done((bf16[32,4224]{1,0:T(8,128)(2,1)S(1)}, bf16[32,4224]{1,0:T(8,128)(2,1)S(1)}, u32[]{:S(2)}, u32[]{:S(2)}) %collective-permute-start.6) | collective-permute-done | bytes 270368 | tf_op jit(solution)/shard_map/ppermute | solution.py:81
  24.1 0.2 collective-permute-done.7.refs_4_.refs_5_
  24.3 0.3 collective-permute-start.13
  24.6 1.5 %collective-permute-start.8 = (bf16[32,4224]{1,0:T(8,128)(2,1)S(1)}, bf16[32,4224]{1,0:T(8,128)(2,1)S(1)}, u32[]{:S(2)}, u32[]{:S(2)}) collective-permute-start(bf16[32,4224]{1,0:T(8,128)(2,1)S(1)} %collective-permute-done.6.refs_2_.refs_3_), channel_id=1, source_target_pairs={{0,16},{4,12},{8,24},{12,4},{16,0},{20,28},{24,8},{28,20},{1,17},{... | collective-permute-start | bytes 811016 | tf_op jit(solution)/shard_map/ppermute | solution.py:81
  26.1 0.5 collective-permute-start.10
  26.6 1.2 %collective-permute-start.12 = (bf16[16,4224]{1,0:T(8,128)(2,1)S(1)}, bf16[16,4224]{1,0:T(8,128)(2,1)S(1)}, u32[]{:S(2)}, u32[]{:S(2)}) collective-permute-start(bf16[16,4224]{1,0:T(8,128)(2,1)S(1)} %collective-permute-done.5.refs_1_), channel_id=1, source_target_pairs={{0,16},{4,12},{8,24},{12,4},{16,0},{20,28},{24,8},{28,20},{1,17},{... | collective-permute-start | bytes 405512 | tf_op jit(solution)/shard_map/ppermute | solution.py:81
  27.8 4.8 %collective-permute-done.10.refs_3_ = bf16[16,4224]{1,0:T(8,128)(2,1)S(1)} collective-permute-done((bf16[16,4224]{1,0:T(8,128)(2,1)S(1)}, bf16[16,4224]{1,0:T(8,128)(2,1)S(1)}, u32[]{:S(2)}, u32[]{:S(2)}) %collective-permute-start.10) | collective-permute-done | bytes 135200 | tf_op jit(solution)/shard_map/ppermute | solution.py:81
  32.6 0.5 collective-permute-start.11
  33.1 3.5 %shard_map.67 = (bf16[2,128,384]{2,1,0:T(8,128)(2,1)S(1)}, f32[2,128,128]{2,1,0:T(8,128)S(1)}) custom-call(bf16[32,4224]{1,0:T(8,128)(2,1)S(1)} %constant_dynamic-update-slice_fusion.refs_0_.refs_1_, bf16[32,4224]{1,0:T(8,128)(2,1)S(1)} %constant_dynamic-update-slice_fusion.refs_0_.refs_1_, bf16[32,4224]{1,0:T(8,128)(2,1)S(1)} %collective-permute-done.6.refs_2_.refs_3_, ...), custom_call_target="tpu_custom_call" | custom-call | flops 1610612736 | bytes 14745600 | tf_op jit(solution)/shard_map/pallas_call | solution.py:201
  36.6 1.0 %collective-permute-done.11.refs_7_ = bf16[16,4224]{1,0:T(8,128)(2,1)S(1)} collective-permute-done((bf16[16,4224]{1,0:T(8,128)(2,1)S(1)}, bf16[16,4224]{1,0:T(8,128)(2,1)S(1)}, u32[]{:S(2)}, u32[]{:S(2)}) %collective-permute-start.11) | collective-permute-done | bytes 135200 | tf_op jit(solution)/shard_map/ppermute | solution.py:81
  37.6 0.6 collective-permute-start.16
  38.3 3.5 %shard_map.68 = (bf16[2,128,384]{2,1,0:T(8,128)(2,1)S(1)}, f32[2,128,128]{2,1,0:T(8,128)S(1)}) custom-call(bf16[16,4224]{1,0:T(8,128)(2,1)S(1)} %copy-done.3, bf16[16,4224]{1,0:T(8,128)(2,1)S(1)} %collective-permute-done.5.refs_1_, bf16[16,4224]{1,0:T(8,128)(2,1)S(1)} %collective-permute-done.2.refs_2_, ...), custom_call_target="tpu_custom_call" | custom-call | flops 1610612736 | bytes 13664256 | tf_op jit(solution)/shard_map/pallas_call | solution.py:201
  41.8 1.5 %collective-permute-start.14 = (bf16[2,128,384]{2,1,0:T(8,128)(2,1)S(1)}, bf16[2,128,384]{2,1,0:T(8,128)(2,1)S(1)}, u32[]{:S(2)}, u32[]{:S(2)}) collective-permute-start(bf16[2,128,384]{2,1,0:T(8,128)(2,1)S(1)} %get-tuple-element.50.own_ref), channel_id=1, source_target_pairs={{0,16},{16,0},{1,17},{17,1},{2,18},{18,2},{3,19},{19,3},{4,20},{20... | collective-permute-start | bytes 589832 | tf_op jit(solution)/shard_map/ppermute | solution.py:74
  43.2 0.1 collective-permute-done.16.other_ref
  43.4 1.1 %shard_map.70 = (f32[64,2048]{1,0:T(8,128)S(1)}, bf16[64,2048]{1,0:T(8,128)(2,1)S(1)}) custom-call(bf16[2,128,384]{2,1,0:T(8,128)(2,1)S(1)} %get-tuple-element.55.own_ref, bf16[2,128,384]{2,1,0:T(8,128)(2,1)S(1)} %collective-permute-done.16.other_ref, f32[2,128,128]{2,1,0:T(8,128)S(1)} %get-tuple-element.56.share_ref, ...), custom_call_target="tpu_custom_call" | custom-call | flops 805306368 | bytes 6815744 | tf_op jit(solution)/shard_map/pallas_call | solution.py:201
  44.5 0.5 collective-permute-start.17
  45.0 2.5 %collective-permute-done.14.other_ref = bf16[2,128,384]{2,1,0:T(8,128)(2,1)S(1)} collective-permute-done((bf16[2,128,384]{2,1,0:T(8,128)(2,1)S(1)}, bf16[2,128,384]{2,1,0:T(8,128)(2,1)S(1)}, u32[]{:S(2)}, u32[]{:S(2)}) %collective-permute-start.14) | collective-permute-done | bytes 196640 | tf_op jit(solution)/shard_map/ppermute | solution.py:74
  47.5 1.0 %shard_map.69 = (f32[32,2048]{1,0:T(8,128)S(1)}, bf16[32,2048]{1,0:T(8,128)(2,1)S(1)}, bf16[32,2048]{1,0:T(8,128)(2,1)S(1)}, bf16[32,2048]{1,0:T(8,128)(2,1)S(1)}) custom-call(bf16[2,128,384]{2,1,0:T(8,128)(2,1)S(1)} %get-tuple-element.50.own_ref, bf16[2,128,384]{2,1,0:T(8,128)(2,1)S(1)} %collective-permute-done.14.other_ref, ...), custom_call_target="tpu_custom_call" | custom-call | flops 805306368 | bytes 6815744 | tf_op jit(solution)/shard_map/pallas_call | solution.py:201
  48.6 1.5 %collective-permute-start.19 = (bf16[32,2048]{1,0:T(8,128)(2,1)S(1)}, bf16[32,2048]{1,0:T(8,128)(2,1)S(1)}, u32[]{:S(2)}, u32[]{:S(2)}) collective-permute-start(bf16[32,2048]{1,0:T(8,128)(2,1)S(1)} %get-tuple-element.59), channel_id=1, source_target_pairs={{0,16},{16,0},{1,17},{17,1},{2,18},{18,2},{3,19},{19,3},{4,20},{20... | collective-permute-start | bytes 393224 | tf_op jit(solution)/shard_map/ppermute | solution.py:74
  50.0 1.2 %collective-permute-start.20 = (bf16[32,2048]{1,0:T(8,128)(2,1)S(1)}, bf16[32,2048]{1,0:T(8,128)(2,1)S(1)}, u32[]{:S(2)}, u32[]{:S(2)}) collective-permute-start(bf16[32,2048]{1,0:T(8,128)(2,1)S(1)} %get-tuple-element.60), channel_id=1, source_target_pairs={{0,24},{4,28},{8,16},{12,20},{16,8},{20,12},{24,0},{28,4},{1,25},{... | collective-permute-start | bytes 393224 | tf_op jit(solution)/shard_map/ppermute | solution.py:74
  51.2 1.3 %collective-permute-done.17 = bf16[64,2048]{1,0:T(8,128)(2,1)S(1)} collective-permute-done((bf16[64,2048]{1,0:T(8,128)(2,1)S(1)}, bf16[64,2048]{1,0:T(8,128)(2,1)S(1)}, u32[]{:S(2)}, u32[]{:S(2)}) %collective-permute-start.17) | collective-permute-done | bytes 262176 | tf_op jit(solution)/shard_map/ppermute | solution.py:74
  52.6 1.0 %collective-permute-start.21 = (bf16[32,2048]{1,0:T(8,128)(2,1)S(1)}, bf16[32,2048]{1,0:T(8,128)(2,1)S(1)}, u32[]{:S(2)}, u32[]{:S(2)}) collective-permute-start(bf16[32,2048]{1,0:T(8,128)(2,1)S(1)} %get-tuple-element.61), channel_id=1, source_target_pairs={{0,17},{1,16},{2,19},{3,18},{16,1},{17,0},{18,3},{19,2},{4,21},{5,... | collective-permute-start | bytes 393224 | tf_op jit(solution)/shard_map/ppermute | solution.py:74
  53.6 1.1 %collective-permute-start.15 = (bf16[32,2048]{1,0:T(8,128)(2,1)S(1)}, bf16[32,2048]{1,0:T(8,128)(2,1)S(1)}, u32[]{:S(2)}, u32[]{:S(2)}) collective-permute-start(bf16[32,2048]{1,0:T(8,128)(2,1)S(1)} %get-tuple-element.54), channel_id=1, source_target_pairs={{0,8},{4,12},{8,0},{12,4},{1,9},{5,13},{9,1},{13,5},{2,10},{6,14},... | collective-permute-start | bytes 393224 | tf_op jit(solution)/shard_map/ppermute | solution.py:74
  54.7 0.8 %collective-permute-start.18 = (bf16[32,2048]{1,0:T(8,128)(2,1)S(1)}, bf16[32,2048]{1,0:T(8,128)(2,1)S(1)}, u32[]{:S(2)}, u32[]{:S(2)}) collective-permute-start(bf16[32,2048]{1,0:T(8,128)(2,1)S(1)} %get-tuple-element.62), channel_id=1, source_target_pairs={{0,1},{1,0},{2,3},{3,2},{4,5},{5,4},{6,7},{7,6},{8,9},{9,8},{10,11... | collective-permute-start | bytes 393224 | tf_op jit(solution)/shard_map/ppermute | solution.py:74
  55.6 2.5 %collective-permute-done.20 = bf16[32,2048]{1,0:T(8,128)(2,1)S(1)} collective-permute-done((bf16[32,2048]{1,0:T(8,128)(2,1)S(1)}, bf16[32,2048]{1,0:T(8,128)(2,1)S(1)}, u32[]{:S(2)}, u32[]{:S(2)}) %collective-permute-start.20) | collective-permute-done | bytes 131104 | tf_op jit(solution)/shard_map/ppermute | solution.py:74
  58.1 0.5 collective-permute-done.21
  58.6 0.3 collective-permute-done.15
  58.9 2.2 %collective-permute-done.18 = bf16[32,2048]{1,0:T(8,128)(2,1)S(1)} collective-permute-done((bf16[32,2048]{1,0:T(8,128)(2,1)S(1)}, bf16[32,2048]{1,0:T(8,128)(2,1)S(1)}, u32[]{:S(2)}, u32[]{:S(2)}) %collective-permute-start.18) | collective-permute-done | bytes 131104 | tf_op jit(solution)/shard_map/ppermute | solution.py:74
  61.2 1.7 %collective-permute-start.22 = (bf16[2,16,2048]{2,1,0:T(8,128)(2,1)S(1)}, bf16[2,16,2048]{2,1,0:T(8,128)(2,1)S(1)}, u32[]{:S(2)}, u32[]{:S(2)}) collective-permute-start(bf16[2,16,2048]{2,1,0:T(8,128)(2,1)S(1)} %fusion.5), channel_id=1, source_target_pairs={{0,2},{1,3},{2,0},{3,1},{4,6},{5,7},{6,4},{7,5},{8,10},{9,11},{10,... | collective-permute-start | bytes 393224 | tf_op jit(solution)/shard_map/ppermute | solution.py:74
  62.8 5.1 %collective-permute-done.22 = bf16[2,16,2048]{2,1,0:T(8,128)(2,1)S(1)} collective-permute-done((bf16[2,16,2048]{2,1,0:T(8,128)(2,1)S(1)}, bf16[2,16,2048]{2,1,0:T(8,128)(2,1)S(1)}, u32[]{:S(2)}, u32[]{:S(2)}) %collective-permute-start.22) | collective-permute-done | bytes 131104 | tf_op jit(solution)/shard_map/ppermute | solution.py:74
  68.0 0.7 %maximum_select_fusion = bf16[16,4096]{1,0:T(8,128)(2,1)} fusion(bf16[16,2048]{1,0:T(8,128)(2,1)S(1)} %get-tuple-element.64, bf16[16,2048]{1,0:T(8,128)(2,1)S(1)} %get-tuple-element.63, pred[]{:T(512)S(6)} %eq.3), kind=kLoop, calls=%fused_computation.12 | loop fusion | flops 589824 | bytes 262145 | tf_op jit(solution)/shard_map/jit(_where)/select_n | solution.py:328
  (23 shorter events, 0.3 us)
Async XLA Ops:
  1.6 8.6 %collective-permute-start.2 = (bf16[16,4224]{1,0:T(8,128)(2,1)}, bf16[16,4224]{1,0:T(8,128)(2,1)S(1)}, u32[]{:S(2)}, u32[]{:S(2)}) collective-permute-start(bf16[16,4224]{1,0:T(8,128)(2,1)} %shard_map.64.refs_0_), channel_id=1, source_target_pairs={{0,8},{4,20},{8,0},{12,28},{16,24},{20,4},{24,16},{28,12},{1,9},{5... | collective-permute-start | bytes 405512 | tf_op jit(solution)/shard_map/ppermute | solution.py:81
  4.6 10.3 %collective-permute-start = (bf16[16,4224]{1,0:T(8,128)(2,1)}, bf16[16,4224]{1,0:T(8,128)(2,1)S(1)}, u32[]{:S(2)}, u32[]{:S(2)}) collective-permute-start(bf16[16,4224]{1,0:T(8,128)(2,1)} %shard_map.64.refs_0_), channel_id=1, source_target_pairs={{0,1},{1,0},{2,3},{3,2},{4,5},{5,4},{6,7},{7,6},{8,9},{9,8},{10,11... | collective-permute-start | bytes 405512 | tf_op jit(solution)/shard_map/ppermute | solution.py:74
  6.2 8.7 %collective-permute-start.1 = (bf16[16,4224]{1,0:T(8,128)(2,1)}, bf16[16,4224]{1,0:T(8,128)(2,1)S(1)}, u32[]{:S(2)}, u32[]{:S(2)}) collective-permute-start(bf16[16,4224]{1,0:T(8,128)(2,1)} %shard_map.64.refs_0_), channel_id=1, source_target_pairs={{0,3},{1,2},{2,1},{3,0},{4,7},{5,6},{6,5},{7,4},{8,11},{9,10},{10,... | collective-permute-start | bytes 405512 | tf_op jit(solution)/shard_map/ppermute | solution.py:74
  8.7 6.3 %collective-permute-start.4 = (bf16[16,4224]{1,0:T(8,128)(2,1)}, bf16[16,4224]{1,0:T(8,128)(2,1)S(1)}, u32[]{:S(2)}, u32[]{:S(2)}) collective-permute-start(bf16[16,4224]{1,0:T(8,128)(2,1)} %shard_map.64.refs_0_), channel_id=1, source_target_pairs={{0,16},{4,12},{8,24},{12,4},{16,0},{20,28},{24,8},{28,20},{1,17},{... | collective-permute-start | bytes 405512 | tf_op jit(solution)/shard_map/ppermute | solution.py:81
  10.2 5.2 %collective-permute-start.3 = (bf16[16,4224]{1,0:T(8,128)(2,1)S(1)}, bf16[16,4224]{1,0:T(8,128)(2,1)S(1)}, u32[]{:S(2)}, u32[]{:S(2)}) collective-permute-start(bf16[16,4224]{1,0:T(8,128)(2,1)S(1)} %collective-permute-done.2.refs_2_), channel_id=1, source_target_pairs={{0,16},{4,12},{8,24},{12,4},{16,0},{20,28},{24,8},{28,20},{1,17},{... | collective-permute-start | bytes 405512 | tf_op jit(solution)/shard_map/ppermute | solution.py:81
  10.7 1.9 %copy-start.1 = (bf16[1,384,4096]{2,1,0:T(8,128)(2,1)S(1)}, bf16[1,384,4096]{2,1,0:T(8,128)(2,1)}, u32[]{:S(2)}) copy-start(bf16[1,384,4096]{2,1,0:T(8,128)(2,1)} %param.9) | copy-start | bytes 9437188
  12.6 1.9 %copy-start.2 = (bf16[1,384,4096]{2,1,0:T(8,128)(2,1)S(1)}, bf16[1,384,4096]{2,1,0:T(8,128)(2,1)}, u32[]{:S(2)}) copy-start(bf16[1,384,4096]{2,1,0:T(8,128)(2,1)} %param.10) | copy-start | bytes 9437188
  14.5 3.6 %copy-start = (bf16[1,768,2048]{2,1,0:T(8,128)(2,1)S(1)}, bf16[1,768,2048]{2,1,0:T(8,128)(2,1)}, u32[]{:S(2)}) copy-start(bf16[1,768,2048]{2,1,0:T(8,128)(2,1)} %param.11) | copy-start | bytes 9437188
  15.3 17.8 %collective-permute-start.9 = (bf16[768,4096]{1,0:T(8,128)(2,1)S(1)}, bf16[768,4096]{1,0:T(8,128)(2,1)S(1)}, u32[]{:S(2)}, u32[]{:S(2)}) collective-permute-start(bf16[768,4096]{1,0:T(8,128)(2,1)S(1)} %shard_map.65.refs_8_), channel_id=1, source_target_pairs={{0,4},{4,0},{8,12},{12,8},{1,5},{5,1},{9,13},{13,9},{2,6},{6,2},{1... | collective-permute-start | bytes 18874376 | tf_op jit(solution)/shard_map/ppermute | solution.py:74
  15.4 8.7 %collective-permute-start.6 = (bf16[32,4224]{1,0:T(8,128)(2,1)S(1)}, bf16[32,4224]{1,0:T(8,128)(2,1)S(1)}, u32[]{:S(2)}, u32[]{:S(2)}) collective-permute-start(bf16[32,4224]{1,0:T(8,128)(2,1)S(1)} %constant_dynamic-update-slice_fusion.refs_0_.refs_1_), channel_id=1, source_target_pairs={{0,8},{4,20},{8,0},{12,28},{16,24},{20,4},{24,16},{28,12},{1,9},{5... | collective-permute-start | bytes 811016 | tf_op jit(solution)/shard_map/ppermute | solution.py:81
  16.5 7.8 %collective-permute-start.7 = (bf16[32,4224]{1,0:T(8,128)(2,1)S(1)}, bf16[32,4224]{1,0:T(8,128)(2,1)S(1)}, u32[]{:S(2)}, u32[]{:S(2)}) collective-permute-start(bf16[32,4224]{1,0:T(8,128)(2,1)S(1)} %constant_dynamic-update-slice_fusion.refs_0_.refs_1_), channel_id=1, source_target_pairs={{0,16},{4,12},{8,24},{12,4},{16,0},{20,28},{24,8},{28,20},{1,17},{... | collective-permute-start | bytes 811016 | tf_op jit(solution)/shard_map/ppermute | solution.py:81
  17.4 5.4 %collective-permute-start.5 = (bf16[16,4224]{1,0:T(8,128)(2,1)S(1)}, bf16[16,4224]{1,0:T(8,128)(2,1)S(1)}, u32[]{:S(2)}, u32[]{:S(2)}) collective-permute-start(bf16[16,4224]{1,0:T(8,128)(2,1)S(1)} %collective-permute-done.1), channel_id=1, source_target_pairs={{0,1},{1,0},{2,3},{3,2},{4,5},{5,4},{6,7},{7,6},{8,9},{9,8},{10,11... | collective-permute-start | bytes 405512 | tf_op jit(solution)/shard_map/ppermute | solution.py:74
  18.4 19.9 %copy-start.3 = (bf16[16,4224]{1,0:T(8,128)(2,1)S(1)}, bf16[16,4224]{1,0:T(8,128)(2,1)}, u32[]{:S(2)}) copy-start(bf16[16,4224]{1,0:T(8,128)(2,1)} %shard_map.64.refs_0_) | copy-start | bytes 405508
  24.3 13.3 %collective-permute-start.13 = (bf16[768,2048]{1,0:T(8,128)(2,1)S(1)}, bf16[768,2048]{1,0:T(8,128)(2,1)S(1)}, u32[]{:S(2)}, u32[]{:S(2)}) collective-permute-start(bf16[768,2048]{1,0:T(8,128)(2,1)S(1)} %shard_map.66.down_own), channel_id=1, source_target_pairs={{0,4},{4,0},{8,12},{12,8},{1,5},{5,1},{9,13},{13,9},{2,6},{6,2},{1... | collective-permute-start | bytes 9437192 | tf_op jit(solution)/shard_map/ppermute | solution.py:74
  24.6 8.5 %collective-permute-start.8 = (bf16[32,4224]{1,0:T(8,128)(2,1)S(1)}, bf16[32,4224]{1,0:T(8,128)(2,1)S(1)}, u32[]{:S(2)}, u32[]{:S(2)}) collective-permute-start(bf16[32,4224]{1,0:T(8,128)(2,1)S(1)} %collective-permute-done.6.refs_2_.refs_3_), channel_id=1, source_target_pairs={{0,16},{4,12},{8,24},{12,4},{16,0},{20,28},{24,8},{28,20},{1,17},{... | collective-permute-start | bytes 811016 | tf_op jit(solution)/shard_map/ppermute | solution.py:81
  26.1 6.5 %collective-permute-start.10 = (bf16[16,4224]{1,0:T(8,128)(2,1)S(1)}, bf16[16,4224]{1,0:T(8,128)(2,1)S(1)}, u32[]{:S(2)}, u32[]{:S(2)}) collective-permute-start(bf16[16,4224]{1,0:T(8,128)(2,1)S(1)} %collective-permute-done.5.refs_1_), channel_id=1, source_target_pairs={{0,8},{4,20},{8,0},{12,28},{16,24},{20,4},{24,16},{28,12},{1,9},{5... | collective-permute-start | bytes 405512 | tf_op jit(solution)/shard_map/ppermute | solution.py:81
  26.6 10.0 %collective-permute-start.12 = (bf16[16,4224]{1,0:T(8,128)(2,1)S(1)}, bf16[16,4224]{1,0:T(8,128)(2,1)S(1)}, u32[]{:S(2)}, u32[]{:S(2)}) collective-permute-start(bf16[16,4224]{1,0:T(8,128)(2,1)S(1)} %collective-permute-done.5.refs_1_), channel_id=1, source_target_pairs={{0,16},{4,12},{8,24},{12,4},{16,0},{20,28},{24,8},{28,20},{1,17},{... | collective-permute-start | bytes 405512 | tf_op jit(solution)/shard_map/ppermute | solution.py:81
  32.6 5.0 %collective-permute-start.11 = (bf16[16,4224]{1,0:T(8,128)(2,1)S(1)}, bf16[16,4224]{1,0:T(8,128)(2,1)S(1)}, u32[]{:S(2)}, u32[]{:S(2)}) collective-permute-start(bf16[16,4224]{1,0:T(8,128)(2,1)S(1)} %collective-permute-done.10.refs_3_), channel_id=1, source_target_pairs={{0,16},{4,12},{8,24},{12,4},{16,0},{20,28},{24,8},{28,20},{1,17},{... | collective-permute-start | bytes 405512 | tf_op jit(solution)/shard_map/ppermute | solution.py:81
  37.6 5.7 %collective-permute-start.16 = (bf16[2,128,384]{2,1,0:T(8,128)(2,1)S(1)}, bf16[2,128,384]{2,1,0:T(8,128)(2,1)S(1)}, u32[]{:S(2)}, u32[]{:S(2)}) collective-permute-start(bf16[2,128,384]{2,1,0:T(8,128)(2,1)S(1)} %get-tuple-element.55.own_ref), channel_id=1, source_target_pairs={{0,16},{16,0},{1,17},{17,1},{2,18},{18,2},{3,19},{19,3},{4,20},{20... | collective-permute-start | bytes 589832 | tf_op jit(solution)/shard_map/ppermute | solution.py:74
  41.8 5.7 %collective-permute-start.14 = (bf16[2,128,384]{2,1,0:T(8,128)(2,1)S(1)}, bf16[2,128,384]{2,1,0:T(8,128)(2,1)S(1)}, u32[]{:S(2)}, u32[]{:S(2)}) collective-permute-start(bf16[2,128,384]{2,1,0:T(8,128)(2,1)S(1)} %get-tuple-element.50.own_ref), channel_id=1, source_target_pairs={{0,16},{16,0},{1,17},{17,1},{2,18},{18,2},{3,19},{19,3},{4,20},{20... | collective-permute-start | bytes 589832 | tf_op jit(solution)/shard_map/ppermute | solution.py:74
  44.5 8.1 %collective-permute-start.17 = (bf16[64,2048]{1,0:T(8,128)(2,1)S(1)}, bf16[64,2048]{1,0:T(8,128)(2,1)S(1)}, u32[]{:S(2)}, u32[]{:S(2)}) collective-permute-start(bf16[64,2048]{1,0:T(8,128)(2,1)S(1)} %get-tuple-element.58), channel_id=1, source_target_pairs={{0,8},{4,12},{8,0},{12,4},{1,9},{5,13},{9,1},{13,5},{2,10},{6,14},... | collective-permute-start | bytes 786440 | tf_op jit(solution)/shard_map/ppermute | solution.py:74
  48.6 7.0 %collective-permute-start.19 = (bf16[32,2048]{1,0:T(8,128)(2,1)S(1)}, bf16[32,2048]{1,0:T(8,128)(2,1)S(1)}, u32[]{:S(2)}, u32[]{:S(2)}) collective-permute-start(bf16[32,2048]{1,0:T(8,128)(2,1)S(1)} %get-tuple-element.59), channel_id=1, source_target_pairs={{0,16},{16,0},{1,17},{17,1},{2,18},{18,2},{3,19},{19,3},{4,20},{20... | collective-permute-start | bytes 393224 | tf_op jit(solution)/shard_map/ppermute | solution.py:74
  50.0 8.0 %collective-permute-start.20 = (bf16[32,2048]{1,0:T(8,128)(2,1)S(1)}, bf16[32,2048]{1,0:T(8,128)(2,1)S(1)}, u32[]{:S(2)}, u32[]{:S(2)}) collective-permute-start(bf16[32,2048]{1,0:T(8,128)(2,1)S(1)} %get-tuple-element.60), channel_id=1, source_target_pairs={{0,24},{4,28},{8,16},{12,20},{16,8},{20,12},{24,0},{28,4},{1,25},{... | collective-permute-start | bytes 393224 | tf_op jit(solution)/shard_map/ppermute | solution.py:74
  52.6 5.9 %collective-permute-start.21 = (bf16[32,2048]{1,0:T(8,128)(2,1)S(1)}, bf16[32,2048]{1,0:T(8,128)(2,1)S(1)}, u32[]{:S(2)}, u32[]{:S(2)}) collective-permute-start(bf16[32,2048]{1,0:T(8,128)(2,1)S(1)} %get-tuple-element.61), channel_id=1, source_target_pairs={{0,17},{1,16},{2,19},{3,18},{16,1},{17,0},{18,3},{19,2},{4,21},{5,... | collective-permute-start | bytes 393224 | tf_op jit(solution)/shard_map/ppermute | solution.py:74
  53.6 5.3 %collective-permute-start.15 = (bf16[32,2048]{1,0:T(8,128)(2,1)S(1)}, bf16[32,2048]{1,0:T(8,128)(2,1)S(1)}, u32[]{:S(2)}, u32[]{:S(2)}) collective-permute-start(bf16[32,2048]{1,0:T(8,128)(2,1)S(1)} %get-tuple-element.54), channel_id=1, source_target_pairs={{0,8},{4,12},{8,0},{12,4},{1,9},{5,13},{9,1},{13,5},{2,10},{6,14},... | collective-permute-start | bytes 393224 | tf_op jit(solution)/shard_map/ppermute | solution.py:74
  54.7 6.3 %collective-permute-start.18 = (bf16[32,2048]{1,0:T(8,128)(2,1)S(1)}, bf16[32,2048]{1,0:T(8,128)(2,1)S(1)}, u32[]{:S(2)}, u32[]{:S(2)}) collective-permute-start(bf16[32,2048]{1,0:T(8,128)(2,1)S(1)} %get-tuple-element.62), channel_id=1, source_target_pairs={{0,1},{1,0},{2,3},{3,2},{4,5},{5,4},{6,7},{7,6},{8,9},{9,8},{10,11... | collective-permute-start | bytes 393224 | tf_op jit(solution)/shard_map/ppermute | solution.py:74
  61.2 6.8 %collective-permute-start.22 = (bf16[2,16,2048]{2,1,0:T(8,128)(2,1)S(1)}, bf16[2,16,2048]{2,1,0:T(8,128)(2,1)S(1)}, u32[]{:S(2)}, u32[]{:S(2)}) collective-permute-start(bf16[2,16,2048]{2,1,0:T(8,128)(2,1)S(1)} %fusion.5), channel_id=1, source_target_pairs={{0,2},{1,3},{2,0},{3,1},{4,6},{5,7},{6,4},{7,5},{8,10},{9,11},{10,... | collective-permute-start | bytes 393224 | tf_op jit(solution)/shard_map/ppermute | solution.py:74

commit v3 on v0

--- a/solution.py
+++ b/solution.py
@@ -321,6 +321,7 @@
     here, there = narrow(keep + wide(back_y)).reshape(2, 2 * row_count, -1)
     there = swap(there, ("rep", "local"), places | 1)
     here = swap(here, "local", 1)
+    across, along_x, there = together((across, along_x, there))
     own = keep_a + wide(along_y) + wide(here)
     other = wide(along_x) + wide(across) + wide(there)
     total = jnp.stack([own, other]).reshape(2, 2, row_count, -1)

time: 68 us -> 70.7 us (1.040)
  waiting for transfers between devices: 21.8 us -> 25.1 us
    ppermute x14, waiting for transfers between devices: 15 us -> 18.2 us  [swap(): lax.ppermute(block, axes, [(place, place ^ mask) for place in range(size)])]
  transfers between devices with their start and end apart: 23 -> 23, of which waited for: 15 -> 14; matrix products, arithmetic and copies ran while one was open for 0% -> 0% of each run, Pallas kernels for 15% -> 14%
where the time goes in v3:
time: 70.7 us; the launch traced here: 70.5 us
  starting transfers between devices  29.1 us (41%)
  waiting for transfers between devices  25.1 us (36%)
  Pallas kernels  11.4 us (16%)
  local copies, waits for them, and re-layouts  3.84 us (5%)
  other arithmetic  0.87 us (1%)
    ppermute x14, waiting for transfers between devices, swap(): lax.ppermute(block, axes, [(place, place ^ mask) for place in range(size)])  18.2 us
    ppermute x14, starting transfers between devices, swap(): lax.ppermute(block, axes, [(place, place ^ mask) for place in range(size)])  18.1 us
    pallas_call x7, Pallas kernels, run(): pl.pallas_call(functools.partial(kernel, **sizes), out_shape=out_shape, i...  11.4 us
    ppermute x9, starting transfers between devices, turn(): return lax.ppermute(block, ('rep', 'node'), pairs)  11.1 us
    ppermute x9, waiting for transfers between devices, turn(): return lax.ppermute(block, ('rep', 'node'), pairs)  6.86 us
    unnamed x9, local copies, waits for them, and re-layouts  3.8 us
  transfers between devices with their start and end apart: 23, of which 14 were waited for; matrix products, arithmetic and copies ran while one was open for 0% of the time, Pallas kernels for 14%

profile of v3, /device:TPU:0, one launch (start us, length us, event | category | flops | bytes accessed | tf_op | source)
XLA Modules:
  0.0 70.5 jit_solution(14591678654361975828)
XLA Ops:
  0.0 1.6 %shard_map.64.refs_0_ = bf16[16,4224]{1,0:T(8,128)(2,1)} custom-call(bf16[16,4096]{1,0:T(8,128)(2,1)} %tokens_in.1, s32[8,16]{1,0:T(8,128)} %bitcast.30, f32[8,16]{1,0:T(8,128)} %bitcast.31), custom_call_target="tpu_custom_call" | custom-call | bytes 132096 | tf_op jit(solution)/shard_map/pallas_call | solution.py:201
  1.6 3.0 %collective-permute-start.2 = (bf16[16,4224]{1,0:T(8,128)(2,1)}, bf16[16,4224]{1,0:T(8,128)(2,1)S(1)}, u32[]{:S(2)}, u32[]{:S(2)}) collective-permute-start(bf16[16,4224]{1,0:T(8,128)(2,1)} %shard_map.64.refs_0_), channel_id=1, source_target_pairs={{0,8},{4,20},{8,0},{12,28},{16,24},{20,4},{24,16},{28,12},{1,9},{5... | collective-permute-start | bytes 405512 | tf_op jit(solution)/shard_map/ppermute | solution.py:81
  4.6 3.6 %collective-permute-start = (bf16[16,4224]{1,0:T(8,128)(2,1)}, bf16[16,4224]{1,0:T(8,128)(2,1)S(1)}, u32[]{:S(2)}, u32[]{:S(2)}) collective-permute-start(bf16[16,4224]{1,0:T(8,128)(2,1)} %shard_map.64.refs_0_), channel_id=1, source_target_pairs={{0,3},{1,2},{2,1},{3,0},{4,7},{5,6},{6,5},{7,4},{8,11},{9,10},{10,... | collective-permute-start | bytes 405512 | tf_op jit(solution)/shard_map/ppermute | solution.py:74
  8.2 1.5 %collective-permute-start.4 = (bf16[16,4224]{1,0:T(8,128)(2,1)}, bf16[16,4224]{1,0:T(8,128)(2,1)S(1)}, u32[]{:S(2)}, u32[]{:S(2)}) collective-permute-start(bf16[16,4224]{1,0:T(8,128)(2,1)} %shard_map.64.refs_0_), channel_id=1, source_target_pairs={{0,16},{4,12},{8,24},{12,4},{16,0},{20,28},{24,8},{28,20},{1,17},{... | collective-permute-start | bytes 405512 | tf_op jit(solution)/shard_map/ppermute | solution.py:81
  9.7 0.0 collective-permute-done.2.refs_2_
  9.7 0.5 collective-permute-start.3
  10.3 1.9 %copy-done.1 = bf16[1,384,4096]{2,1,0:T(8,128)(2,1)S(1)} copy-done((bf16[1,384,4096]{2,1,0:T(8,128)(2,1)S(1)}, bf16[1,384,4096]{2,1,0:T(8,128)(2,1)}, u32[]{:S(2)}) %copy-start.1) | copy-done | bytes 3145752
  12.2 1.9 %copy-done.2 = bf16[1,384,4096]{2,1,0:T(8,128)(2,1)S(1)} copy-done((bf16[1,384,4096]{2,1,0:T(8,128)(2,1)S(1)}, bf16[1,384,4096]{2,1,0:T(8,128)(2,1)}, u32[]{:S(2)}) %copy-start.2) | copy-done | bytes 3145752
  14.0 0.4 shard_map.65.refs_8_
  14.5 0.0 collective-permute-done
  14.5 0.2 collective-permute-done.1
  14.7 0.0 collective-permute-done.4.refs_4_
  14.7 0.2 collective-permute-done.3.refs_6_
  14.9 0.0 collective-permute-start.9
  14.9 1.5 %collective-permute-start.6 = (bf16[32,4224]{1,0:T(8,128)(2,1)S(1)}, bf16[32,4224]{1,0:T(8,128)(2,1)S(1)}, u32[]{:S(2)}, u32[]{:S(2)}) collective-permute-start(bf16[32,4224]{1,0:T(8,128)(2,1)S(1)} %constant_dynamic-update-slice_fusion.refs_0_.refs_1_), channel_id=1, source_target_pairs={{0,8},{4,20},{8,0},{12,28},{16,24},{20,4},{24,16},{28,12},{1,9},{5... | collective-permute-start | bytes 811016 | tf_op jit(solution)/shard_map/ppermute | solution.py:81
  16.4 0.6 collective-permute-start.7
  17.0 2.0 %collective-permute-start.5 = (bf16[16,4224]{1,0:T(8,128)(2,1)S(1)}, bf16[16,4224]{1,0:T(8,128)(2,1)S(1)}, u32[]{:S(2)}, u32[]{:S(2)}) collective-permute-start(bf16[16,4224]{1,0:T(8,128)(2,1)S(1)} %collective-permute-done), channel_id=1, source_target_pairs={{0,1},{1,0},{2,3},{3,2},{4,5},{5,4},{6,7},{7,6},{8,9},{9,8},{10,11... | collective-permute-start | bytes 405512 | tf_op jit(solution)/shard_map/ppermute | solution.py:74
  19.0 0.2 shard_map.66.down_own
  19.3 3.5 %collective-permute-done.5.refs_1_ = bf16[16,4224]{1,0:T(8,128)(2,1)S(1)} collective-permute-done((bf16[16,4224]{1,0:T(8,128)(2,1)S(1)}, bf16[16,4224]{1,0:T(8,128)(2,1)S(1)}, u32[]{:S(2)}, u32[]{:S(2)}) %collective-permute-start.5) | collective-permute-done | bytes 135200 | tf_op jit(solution)/shard_map/ppermute | solution.py:74
  22.7 0.9 %collective-permute-done.6.refs_2_.refs_3_ = bf16[32,4224]{1,0:T(8,128)(2,1)S(1)} collective-permute-done((bf16[32,4224]{1,0:T(8,128)(2,1)S(1)}, bf16[32,4224]{1,0:T(8,128)(2,1)S(1)}, u32[]{:S(2)}, u32[]{:S(2)}) %collective-permute-start.6) | collective-permute-done | bytes 270368 | tf_op jit(solution)/shard_map/ppermute | solution.py:81
  23.6 0.2 collective-permute-done.7.refs_4_.refs_5_
  23.9 0.3 collective-permute-start.13
  24.2 1.5 %collective-permute-start.8 = (bf16[32,4224]{1,0:T(8,128)(2,1)S(1)}, bf16[32,4224]{1,0:T(8,128)(2,1)S(1)}, u32[]{:S(2)}, u32[]{:S(2)}) collective-permute-start(bf16[32,4224]{1,0:T(8,128)(2,1)S(1)} %collective-permute-done.6.refs_2_.refs_3_), channel_id=1, source_target_pairs={{0,16},{4,12},{8,24},{12,4},{16,0},{20,28},{24,8},{28,20},{1,17},{... | collective-permute-start | bytes 811016 | tf_op jit(solution)/shard_map/ppermute | solution.py:81
  25.7 0.5 collective-permute-start.10
  26.2 1.5 %collective-permute-start.12 = (bf16[16,4224]{1,0:T(8,128)(2,1)S(1)}, bf16[16,4224]{1,0:T(8,128)(2,1)S(1)}, u32[]{:S(2)}, u32[]{:S(2)}) collective-permute-start(bf16[16,4224]{1,0:T(8,128)(2,1)S(1)} %collective-permute-done.5.refs_1_), channel_id=1, source_target_pairs={{0,16},{4,12},{8,24},{12,4},{16,0},{20,28},{24,8},{28,20},{1,17},{... | collective-permute-start | bytes 405512 | tf_op jit(solution)/shard_map/ppermute | solution.py:81
  27.6 4.5 %collective-permute-done.10.refs_3_ = bf16[16,4224]{1,0:T(8,128)(2,1)S(1)} collective-permute-done((bf16[16,4224]{1,0:T(8,128)(2,1)S(1)}, bf16[16,4224]{1,0:T(8,128)(2,1)S(1)}, u32[]{:S(2)}, u32[]{:S(2)}) %collective-permute-start.10) | collective-permute-done | bytes 135200 | tf_op jit(solution)/shard_map/ppermute | solution.py:81
  32.2 0.5 collective-permute-start.11
  32.7 0.0 collective-permute-done.8.refs_6_.refs_7_
  32.7 3.5 %shard_map.67 = (bf16[2,128,384]{2,1,0:T(8,128)(2,1)S(1)}, f32[2,128,128]{2,1,0:T(8,128)S(1)}) custom-call(bf16[32,4224]{1,0:T(8,128)(2,1)S(1)} %constant_dynamic-update-slice_fusion.refs_0_.refs_1_, bf16[32,4224]{1,0:T(8,128)(2,1)S(1)} %constant_dynamic-update-slice_fusion.refs_0_.refs_1_, bf16[32,4224]{1,0:T(8,128)(2,1)S(1)} %collective-permute-done.6.refs_2_.refs_3_, ...), custom_call_target="tpu_custom_call" | custom-call | flops 1610612736 | bytes 14745600 | tf_op jit(solution)/shard_map/pallas_call | solution.py:201
  36.2 1.0 %collective-permute-done.11.refs_7_ = bf16[16,4224]{1,0:T(8,128)(2,1)S(1)} collective-permute-done((bf16[16,4224]{1,0:T(8,128)(2,1)S(1)}, bf16[16,4224]{1,0:T(8,128)(2,1)S(1)}, u32[]{:S(2)}, u32[]{:S(2)}) %collective-permute-start.11) | collective-permute-done | bytes 135200 | tf_op jit(solution)/shard_map/ppermute | solution.py:81
  37.2 0.6 collective-permute-start.16
  37.8 3.5 %shard_map.68 = (bf16[2,128,384]{2,1,0:T(8,128)(2,1)S(1)}, f32[2,128,128]{2,1,0:T(8,128)S(1)}) custom-call(bf16[16,4224]{1,0:T(8,128)(2,1)S(1)} %copy-done.3, bf16[16,4224]{1,0:T(8,128)(2,1)S(1)} %collective-permute-done.5.refs_1_, bf16[16,4224]{1,0:T(8,128)(2,1)S(1)} %collective-permute-done.2.refs_2_, ...), custom_call_target="tpu_custom_call" | custom-call | flops 1610612736 | bytes 13664256 | tf_op jit(solution)/shard_map/pallas_call | solution.py:201
  41.3 1.5 %collective-permute-start.14 = (bf16[2,128,384]{2,1,0:T(8,128)(2,1)S(1)}, bf16[2,128,384]{2,1,0:T(8,128)(2,1)S(1)}, u32[]{:S(2)}, u32[]{:S(2)}) collective-permute-start(bf16[2,128,384]{2,1,0:T(8,128)(2,1)S(1)} %get-tuple-element.53.own_ref), channel_id=1, source_target_pairs={{0,16},{16,0},{1,17},{17,1},{2,18},{18,2},{3,19},{19,3},{4,20},{20... | collective-permute-start | bytes 589832 | tf_op jit(solution)/shard_map/ppermute | solution.py:74
  42.8 0.1 collective-permute-done.16.other_ref
  42.9 1.1 %shard_map.70 = (f32[64,2048]{1,0:T(8,128)S(1)}, bf16[64,2048]{1,0:T(8,128)(2,1)S(1)}) custom-call(bf16[2,128,384]{2,1,0:T(8,128)(2,1)S(1)} %get-tuple-element.58.own_ref, bf16[2,128,384]{2,1,0:T(8,128)(2,1)S(1)} %collective-permute-done.16.other_ref, f32[2,128,128]{2,1,0:T(8,128)S(1)} %get-tuple-element.59.share_ref, ...), custom_call_target="tpu_custom_call" | custom-call | flops 805306368 | bytes 6815744 | tf_op jit(solution)/shard_map/pallas_call | solution.py:201
  44.0 1.1 %collective-permute-start.17 = (bf16[64,2048]{1,0:T(8,128)(2,1)S(1)}, bf16[64,2048]{1,0:T(8,128)(2,1)S(1)}, u32[]{:S(2)}, u32[]{:S(2)}) collective-permute-start(bf16[64,2048]{1,0:T(8,128)(2,1)S(1)} %get-tuple-element.61), channel_id=1, source_target_pairs={{0,8},{4,12},{8,0},{12,4},{1,9},{5,13},{9,1},{13,5},{2,10},{6,14},... | collective-permute-start | bytes 786440 | tf_op jit(solution)/shard_map/ppermute | solution.py:74
  45.1 2.0 %collective-permute-done.14.other_ref = bf16[2,128,384]{2,1,0:T(8,128)(2,1)S(1)} collective-permute-done((bf16[2,128,384]{2,1,0:T(8,128)(2,1)S(1)}, bf16[2,128,384]{2,1,0:T(8,128)(2,1)S(1)}, u32[]{:S(2)}, u32[]{:S(2)}) %collective-permute-start.14) | collective-permute-done | bytes 196640 | tf_op jit(solution)/shard_map/ppermute | solution.py:74
  47.1 1.1 %shard_map.69 = (f32[32,2048]{1,0:T(8,128)S(1)}, bf16[32,2048]{1,0:T(8,128)(2,1)S(1)}, bf16[32,2048]{1,0:T(8,128)(2,1)S(1)}, bf16[32,2048]{1,0:T(8,128)(2,1)S(1)}) custom-call(bf16[2,128,384]{2,1,0:T(8,128)(2,1)S(1)} %get-tuple-element.53.own_ref, bf16[2,128,384]{2,1,0:T(8,128)(2,1)S(1)} %collective-permute-done.14.other_ref, ...), custom_call_target="tpu_custom_call" | custom-call | flops 805306368 | bytes 6815744 | tf_op jit(solution)/shard_map/pallas_call | solution.py:201
  48.1 1.5 %collective-permute-start.19 = (bf16[32,2048]{1,0:T(8,128)(2,1)S(1)}, bf16[32,2048]{1,0:T(8,128)(2,1)S(1)}, u32[]{:S(2)}, u32[]{:S(2)}) collective-permute-start(bf16[32,2048]{1,0:T(8,128)(2,1)S(1)} %get-tuple-element.62), channel_id=1, source_target_pairs={{0,24},{4,28},{8,16},{12,20},{16,8},{20,12},{24,0},{28,4},{1,25},{... | collective-permute-start | bytes 393224 | tf_op jit(solution)/shard_map/ppermute | solution.py:74
  49.6 1.4 %collective-permute-start.20 = (bf16[32,2048]{1,0:T(8,128)(2,1)S(1)}, bf16[32,2048]{1,0:T(8,128)(2,1)S(1)}, u32[]{:S(2)}, u32[]{:S(2)}) collective-permute-start(bf16[32,2048]{1,0:T(8,128)(2,1)S(1)} %get-tuple-element.63), channel_id=1, source_target_pairs={{0,16},{16,0},{1,17},{17,1},{2,18},{18,2},{3,19},{19,3},{4,20},{20... | collective-permute-start | bytes 393224 | tf_op jit(solution)/shard_map/ppermute | solution.py:74
  51.0 0.8 %collective-permute-done.17 = bf16[64,2048]{1,0:T(8,128)(2,1)S(1)} collective-permute-done((bf16[64,2048]{1,0:T(8,128)(2,1)S(1)}, bf16[64,2048]{1,0:T(8,128)(2,1)S(1)}, u32[]{:S(2)}, u32[]{:S(2)}) %collective-permute-start.17) | collective-permute-done | bytes 262176 | tf_op jit(solution)/shard_map/ppermute | solution.py:74
  51.9 4.3 %collective-permute-start.21 = (bf16[32,2048]{1,0:T(8,128)(2,1)S(1)}, bf16[32,2048]{1,0:T(8,128)(2,1)S(1)}, u32[]{:S(2)}, u32[]{:S(2)}) collective-permute-start(bf16[32,2048]{1,0:T(8,128)(2,1)S(1)} %get-tuple-element.67), channel_id=1, source_target_pairs={{0,17},{1,16},{2,19},{3,18},{16,1},{17,0},{18,3},{19,2},{4,21},{5,... | collective-permute-start | bytes 393224 | tf_op jit(solution)/shard_map/ppermute | solution.py:74
  56.2 2.9 %collective-permute-done.21 = bf16[32,2048]{1,0:T(8,128)(2,1)S(1)} collective-permute-done((bf16[32,2048]{1,0:T(8,128)(2,1)S(1)}, bf16[32,2048]{1,0:T(8,128)(2,1)S(1)}, u32[]{:S(2)}, u32[]{:S(2)}) %collective-permute-start.21) | collective-permute-done | bytes 131104 | tf_op jit(solution)/shard_map/ppermute | solution.py:74
  59.2 2.0 %collective-permute-done.15 = bf16[32,2048]{1,0:T(8,128)(2,1)S(1)} collective-permute-done((bf16[32,2048]{1,0:T(8,128)(2,1)S(1)}, bf16[32,2048]{1,0:T(8,128)(2,1)S(1)}, u32[]{:S(2)}, u32[]{:S(2)}) %collective-permute-start.15) | collective-permute-done | bytes 131104 | tf_op jit(solution)/shard_map/ppermute | solution.py:74
  61.2 1.2 %collective-permute-done.18 = bf16[32,2048]{1,0:T(8,128)(2,1)S(1)} collective-permute-done((bf16[32,2048]{1,0:T(8,128)(2,1)S(1)}, bf16[32,2048]{1,0:T(8,128)(2,1)S(1)}, u32[]{:S(2)}, u32[]{:S(2)}) %collective-permute-start.18) | collective-permute-done | bytes 131104 | tf_op jit(solution)/shard_map/ppermute | solution.py:74
  62.4 1.8 %collective-permute-start.22 = (bf16[2,16,2048]{2,1,0:T(8,128)(2,1)S(1)}, bf16[2,16,2048]{2,1,0:T(8,128)(2,1)S(1)}, u32[]{:S(2)}, u32[]{:S(2)}) collective-permute-start(bf16[2,16,2048]{2,1,0:T(8,128)(2,1)S(1)} %fusion.5), channel_id=1, source_target_pairs={{0,2},{1,3},{2,0},{3,1},{4,6},{5,7},{6,4},{7,5},{8,10},{9,11},{10,... | collective-permute-start | bytes 393224 | tf_op jit(solution)/shard_map/ppermute | solution.py:74
  64.2 5.6 %collective-permute-done.22 = bf16[2,16,2048]{2,1,0:T(8,128)(2,1)S(1)} collective-permute-done((bf16[2,16,2048]{2,1,0:T(8,128)(2,1)S(1)}, bf16[2,16,2048]{2,1,0:T(8,128)(2,1)S(1)}, u32[]{:S(2)}, u32[]{:S(2)}) %collective-permute-start.22) | collective-permute-done | bytes 131104 | tf_op jit(solution)/shard_map/ppermute | solution.py:74
  69.8 0.7 maximum_select_fusion
  (23 shorter events, 0.3 us)
Async XLA Ops:
  1.6 8.1 %collective-permute-start.2 = (bf16[16,4224]{1,0:T(8,128)(2,1)}, bf16[16,4224]{1,0:T(8,128)(2,1)S(1)}, u32[]{:S(2)}, u32[]{:S(2)}) collective-permute-start(bf16[16,4224]{1,0:T(8,128)(2,1)} %shard_map.64.refs_0_), channel_id=1, source_target_pairs={{0,8},{4,20},{8,0},{12,28},{16,24},{20,4},{24,16},{28,12},{1,9},{5... | collective-permute-start | bytes 405512 | tf_op jit(solution)/shard_map/ppermute | solution.py:81
  4.6 9.9 %collective-permute-start = (bf16[16,4224]{1,0:T(8,128)(2,1)}, bf16[16,4224]{1,0:T(8,128)(2,1)S(1)}, u32[]{:S(2)}, u32[]{:S(2)}) collective-permute-start(bf16[16,4224]{1,0:T(8,128)(2,1)} %shard_map.64.refs_0_), channel_id=1, source_target_pairs={{0,3},{1,2},{2,1},{3,0},{4,7},{5,6},{6,5},{7,4},{8,11},{9,10},{10,... | collective-permute-start | bytes 405512 | tf_op jit(solution)/shard_map/ppermute | solution.py:74
  8.2 6.5 %collective-permute-start.1 = (bf16[16,4224]{1,0:T(8,128)(2,1)}, bf16[16,4224]{1,0:T(8,128)(2,1)S(1)}, u32[]{:S(2)}, u32[]{:S(2)}) collective-permute-start(bf16[16,4224]{1,0:T(8,128)(2,1)} %shard_map.64.refs_0_), channel_id=1, source_target_pairs={{0,1},{1,0},{2,3},{3,2},{4,5},{5,4},{6,7},{7,6},{8,9},{9,8},{10,11... | collective-permute-start | bytes 405512 | tf_op jit(solution)/shard_map/ppermute | solution.py:74
  8.2 6.5 %collective-permute-start.4 = (bf16[16,4224]{1,0:T(8,128)(2,1)}, bf16[16,4224]{1,0:T(8,128)(2,1)S(1)}, u32[]{:S(2)}, u32[]{:S(2)}) collective-permute-start(bf16[16,4224]{1,0:T(8,128)(2,1)} %shard_map.64.refs_0_), channel_id=1, source_target_pairs={{0,16},{4,12},{8,24},{12,4},{16,0},{20,28},{24,8},{28,20},{1,17},{... | collective-permute-start | bytes 405512 | tf_op jit(solution)/shard_map/ppermute | solution.py:81
  9.7 5.2 %collective-permute-start.3 = (bf16[16,4224]{1,0:T(8,128)(2,1)S(1)}, bf16[16,4224]{1,0:T(8,128)(2,1)S(1)}, u32[]{:S(2)}, u32[]{:S(2)}) collective-permute-start(bf16[16,4224]{1,0:T(8,128)(2,1)S(1)} %collective-permute-done.2.refs_2_), channel_id=1, source_target_pairs={{0,16},{4,12},{8,24},{12,4},{16,0},{20,28},{24,8},{28,20},{1,17},{... | collective-permute-start | bytes 405512 | tf_op jit(solution)/shard_map/ppermute | solution.py:81
  10.3 1.9 %copy-start.1 = (bf16[1,384,4096]{2,1,0:T(8,128)(2,1)S(1)}, bf16[1,384,4096]{2,1,0:T(8,128)(2,1)}, u32[]{:S(2)}) copy-start(bf16[1,384,4096]{2,1,0:T(8,128)(2,1)} %param.9) | copy-start | bytes 9437188
  12.1 1.9 %copy-start.2 = (bf16[1,384,4096]{2,1,0:T(8,128)(2,1)S(1)}, bf16[1,384,4096]{2,1,0:T(8,128)(2,1)}, u32[]{:S(2)}) copy-start(bf16[1,384,4096]{2,1,0:T(8,128)(2,1)} %param.10) | copy-start | bytes 9437188
  14.0 5.0 %copy-start = (bf16[1,768,2048]{2,1,0:T(8,128)(2,1)S(1)}, bf16[1,768,2048]{2,1,0:T(8,128)(2,1)}, u32[]{:S(2)}) copy-start(bf16[1,768,2048]{2,1,0:T(8,128)(2,1)} %param.11) | copy-start | bytes 9437188
  14.9 17.8 %collective-permute-start.9 = (bf16[768,4096]{1,0:T(8,128)(2,1)S(1)}, bf16[768,4096]{1,0:T(8,128)(2,1)S(1)}, u32[]{:S(2)}, u32[]{:S(2)}) collective-permute-start(bf16[768,4096]{1,0:T(8,128)(2,1)S(1)} %shard_map.65.refs_8_), channel_id=1, source_target_pairs={{0,4},{4,0},{8,12},{12,8},{1,5},{5,1},{9,13},{13,9},{2,6},{6,2},{1... | collective-permute-start | bytes 18874376 | tf_op jit(solution)/shard_map/ppermute | solution.py:74
  14.9 8.7 %collective-permute-start.6 = (bf16[32,4224]{1,0:T(8,128)(2,1)S(1)}, bf16[32,4224]{1,0:T(8,128)(2,1)S(1)}, u32[]{:S(2)}, u32[]{:S(2)}) collective-permute-start(bf16[32,4224]{1,0:T(8,128)(2,1)S(1)} %constant_dynamic-update-slice_fusion.refs_0_.refs_1_), channel_id=1, source_target_pairs={{0,8},{4,20},{8,0},{12,28},{16,24},{20,4},{24,16},{28,12},{1,9},{5... | collective-permute-start | bytes 811016 | tf_op jit(solution)/shard_map/ppermute | solution.py:81
  16.4 7.5 %collective-permute-start.7 = (bf16[32,4224]{1,0:T(8,128)(2,1)S(1)}, bf16[32,4224]{1,0:T(8,128)(2,1)S(1)}, u32[]{:S(2)}, u32[]{:S(2)}) collective-permute-start(bf16[32,4224]{1,0:T(8,128)(2,1)S(1)} %constant_dynamic-update-slice_fusion.refs_0_.refs_1_), channel_id=1, source_target_pairs={{0,16},{4,12},{8,24},{12,4},{16,0},{20,28},{24,8},{28,20},{1,17},{... | collective-permute-start | bytes 811016 | tf_op jit(solution)/shard_map/ppermute | solution.py:81
  17.0 5.7 %collective-permute-start.5 = (bf16[16,4224]{1,0:T(8,128)(2,1)S(1)}, bf16[16,4224]{1,0:T(8,128)(2,1)S(1)}, u32[]{:S(2)}, u32[]{:S(2)}) collective-permute-start(bf16[16,4224]{1,0:T(8,128)(2,1)S(1)} %collective-permute-done), channel_id=1, source_target_pairs={{0,1},{1,0},{2,3},{3,2},{4,5},{5,4},{6,7},{7,6},{8,9},{9,8},{10,11... | collective-permute-start | bytes 405512 | tf_op jit(solution)/shard_map/ppermute | solution.py:74
  19.3 18.6 %copy-start.3 = (bf16[16,4224]{1,0:T(8,128)(2,1)S(1)}, bf16[16,4224]{1,0:T(8,128)(2,1)}, u32[]{:S(2)}) copy-start(bf16[16,4224]{1,0:T(8,128)(2,1)} %shard_map.64.refs_0_) | copy-start | bytes 405508
  23.9 13.3 %collective-permute-start.13 = (bf16[768,2048]{1,0:T(8,128)(2,1)S(1)}, bf16[768,2048]{1,0:T(8,128)(2,1)S(1)}, u32[]{:S(2)}, u32[]{:S(2)}) collective-permute-start(bf16[768,2048]{1,0:T(8,128)(2,1)S(1)} %shard_map.66.down_own), channel_id=1, source_target_pairs={{0,4},{4,0},{8,12},{12,8},{1,5},{5,1},{9,13},{13,9},{2,6},{6,2},{1... | collective-permute-start | bytes 9437192 | tf_op jit(solution)/shard_map/ppermute | solution.py:74
  24.2 8.5 %collective-permute-start.8 = (bf16[32,4224]{1,0:T(8,128)(2,1)S(1)}, bf16[32,4224]{1,0:T(8,128)(2,1)S(1)}, u32[]{:S(2)}, u32[]{:S(2)}) collective-permute-start(bf16[32,4224]{1,0:T(8,128)(2,1)S(1)} %collective-permute-done.6.refs_2_.refs_3_), channel_id=1, source_target_pairs={{0,16},{4,12},{8,24},{12,4},{16,0},{20,28},{24,8},{28,20},{1,17},{... | collective-permute-start | bytes 811016 | tf_op jit(solution)/shard_map/ppermute | solution.py:81
  25.7 6.5 %collective-permute-start.10 = (bf16[16,4224]{1,0:T(8,128)(2,1)S(1)}, bf16[16,4224]{1,0:T(8,128)(2,1)S(1)}, u32[]{:S(2)}, u32[]{:S(2)}) collective-permute-start(bf16[16,4224]{1,0:T(8,128)(2,1)S(1)} %collective-permute-done.5.refs_1_), channel_id=1, source_target_pairs={{0,8},{4,20},{8,0},{12,28},{16,24},{20,4},{24,16},{28,12},{1,9},{5... | collective-permute-start | bytes 405512 | tf_op jit(solution)/shard_map/ppermute | solution.py:81
  26.2 10.0 %collective-permute-start.12 = (bf16[16,4224]{1,0:T(8,128)(2,1)S(1)}, bf16[16,4224]{1,0:T(8,128)(2,1)S(1)}, u32[]{:S(2)}, u32[]{:S(2)}) collective-permute-start(bf16[16,4224]{1,0:T(8,128)(2,1)S(1)} %collective-permute-done.5.refs_1_), channel_id=1, source_target_pairs={{0,16},{4,12},{8,24},{12,4},{16,0},{20,28},{24,8},{28,20},{1,17},{... | collective-permute-start | bytes 405512 | tf_op jit(solution)/shard_map/ppermute | solution.py:81
  32.2 5.0 %collective-permute-start.11 = (bf16[16,4224]{1,0:T(8,128)(2,1)S(1)}, bf16[16,4224]{1,0:T(8,128)(2,1)S(1)}, u32[]{:S(2)}, u32[]{:S(2)}) collective-permute-start(bf16[16,4224]{1,0:T(8,128)(2,1)S(1)} %collective-permute-done.10.refs_3_), channel_id=1, source_target_pairs={{0,16},{4,12},{8,24},{12,4},{16,0},{20,28},{24,8},{28,20},{1,17},{... | collective-permute-start | bytes 405512 | tf_op jit(solution)/shard_map/ppermute | solution.py:81
  37.2 5.7 %collective-permute-start.16 = (bf16[2,128,384]{2,1,0:T(8,128)(2,1)S(1)}, bf16[2,128,384]{2,1,0:T(8,128)(2,1)S(1)}, u32[]{:S(2)}, u32[]{:S(2)}) collective-permute-start(bf16[2,128,384]{2,1,0:T(8,128)(2,1)S(1)} %get-tuple-element.58.own_ref), channel_id=1, source_target_pairs={{0,16},{16,0},{1,17},{17,1},{2,18},{18,2},{3,19},{19,3},{4,20},{20... | collective-permute-start | bytes 589832 | tf_op jit(solution)/shard_map/ppermute | solution.py:74
  41.3 5.7 %collective-permute-start.14 = (bf16[2,128,384]{2,1,0:T(8,128)(2,1)S(1)}, bf16[2,128,384]{2,1,0:T(8,128)(2,1)S(1)}, u32[]{:S(2)}, u32[]{:S(2)}) collective-permute-start(bf16[2,128,384]{2,1,0:T(8,128)(2,1)S(1)} %get-tuple-element.53.own_ref), channel_id=1, source_target_pairs={{0,16},{16,0},{1,17},{17,1},{2,18},{18,2},{3,19},{19,3},{4,20},{20... | collective-permute-start | bytes 589832 | tf_op jit(solution)/shard_map/ppermute | solution.py:74
  44.0 7.8 %collective-permute-start.17 = (bf16[64,2048]{1,0:T(8,128)(2,1)S(1)}, bf16[64,2048]{1,0:T(8,128)(2,1)S(1)}, u32[]{:S(2)}, u32[]{:S(2)}) collective-permute-start(bf16[64,2048]{1,0:T(8,128)(2,1)S(1)} %get-tuple-element.61), channel_id=1, source_target_pairs={{0,8},{4,12},{8,0},{12,4},{1,9},{5,13},{9,1},{13,5},{2,10},{6,14},... | collective-permute-start | bytes 786440 | tf_op jit(solution)/shard_map/ppermute | solution.py:74
  48.1 8.1 %collective-permute-start.19 = (bf16[32,2048]{1,0:T(8,128)(2,1)S(1)}, bf16[32,2048]{1,0:T(8,128)(2,1)S(1)}, u32[]{:S(2)}, u32[]{:S(2)}) collective-permute-start(bf16[32,2048]{1,0:T(8,128)(2,1)S(1)} %get-tuple-element.62), channel_id=1, source_target_pairs={{0,24},{4,28},{8,16},{12,20},{16,8},{20,12},{24,0},{28,4},{1,25},{... | collective-permute-start | bytes 393224 | tf_op jit(solution)/shard_map/ppermute | solution.py:74
  49.6 6.6 %collective-permute-start.20 = (bf16[32,2048]{1,0:T(8,128)(2,1)S(1)}, bf16[32,2048]{1,0:T(8,128)(2,1)S(1)}, u32[]{:S(2)}, u32[]{:S(2)}) collective-permute-start(bf16[32,2048]{1,0:T(8,128)(2,1)S(1)} %get-tuple-element.63), channel_id=1, source_target_pairs={{0,16},{16,0},{1,17},{17,1},{2,18},{18,2},{3,19},{19,3},{4,20},{20... | collective-permute-start | bytes 393224 | tf_op jit(solution)/shard_map/ppermute | solution.py:74
  51.9 7.2 %collective-permute-start.21 = (bf16[32,2048]{1,0:T(8,128)(2,1)S(1)}, bf16[32,2048]{1,0:T(8,128)(2,1)S(1)}, u32[]{:S(2)}, u32[]{:S(2)}) collective-permute-start(bf16[32,2048]{1,0:T(8,128)(2,1)S(1)} %get-tuple-element.67), channel_id=1, source_target_pairs={{0,17},{1,16},{2,19},{3,18},{16,1},{17,0},{18,3},{19,2},{4,21},{5,... | collective-permute-start | bytes 393224 | tf_op jit(solution)/shard_map/ppermute | solution.py:74
  56.2 5.0 %collective-permute-start.15 = (bf16[32,2048]{1,0:T(8,128)(2,1)S(1)}, bf16[32,2048]{1,0:T(8,128)(2,1)S(1)}, u32[]{:S(2)}, u32[]{:S(2)}) collective-permute-start(bf16[32,2048]{1,0:T(8,128)(2,1)S(1)} %get-tuple-element.57), channel_id=1, source_target_pairs={{0,8},{4,12},{8,0},{12,4},{1,9},{5,13},{9,1},{13,5},{2,10},{6,14},... | collective-permute-start | bytes 393224 | tf_op jit(solution)/shard_map/ppermute | solution.py:74
  56.2 6.1 %collective-permute-start.18 = (bf16[32,2048]{1,0:T(8,128)(2,1)S(1)}, bf16[32,2048]{1,0:T(8,128)(2,1)S(1)}, u32[]{:S(2)}, u32[]{:S(2)}) collective-permute-start(bf16[32,2048]{1,0:T(8,128)(2,1)S(1)} %get-tuple-element.68), channel_id=1, source_target_pairs={{0,1},{1,0},{2,3},{3,2},{4,5},{5,4},{6,7},{7,6},{8,9},{9,8},{10,11... | collective-permute-start | bytes 393224 | tf_op jit(solution)/shard_map/ppermute | solution.py:74
  62.4 7.3 %collective-permute-start.22 = (bf16[2,16,2048]{2,1,0:T(8,128)(2,1)S(1)}, bf16[2,16,2048]{2,1,0:T(8,128)(2,1)S(1)}, u32[]{:S(2)}, u32[]{:S(2)}) collective-permute-start(bf16[2,16,2048]{2,1,0:T(8,128)(2,1)S(1)} %fusion.5), channel_id=1, source_target_pairs={{0,2},{1,3},{2,0},{3,1},{4,6},{5,7},{6,4},{7,5},{8,10},{9,11},{10,... | collective-permute-start | bytes 393224 | tf_op jit(solution)/shard_map/ppermute | solution.py:74
